TPU v7x, 256 devices: a whole 4x4x8 slice. The times are simulated.
256 devices in a mesh: rows: 16 (over z_hi, y), cols: 16 (over z_lo, x, core).
Axes of the slice: x: 4, y: 4, z: 8 (z_hi: 4, z_lo: 2; z = z_hi * 2 + z_lo), core: 2. Of those that a mesh axis runs over, the one named last changes fastest.
Arguments:
- features: bfloat16 [65536, 256], P(('cols', 'rows')), may hold values from -6 to 6
- weight: bfloat16 [256, 256], replicated, may hold values from -0.375 to 0.375
- tile_values: bfloat16 [16, 16, 768, 4096], P('rows', 'cols'), may hold values from -0.0546875 to 0.0546875
- tile_rows: int32 [16, 16, 768], P('rows', 'cols'), may hold values from 0 to 63
- tile_cols: int32 [16, 16, 768], P('rows', 'cols'), may hold values from 0 to 63
- tile_count: int32 [16, 16], P('rows', 'cols'), may hold values from 1 to 768, as said below
- out_grad: bfloat16 [65536, 256], P(('rows', 'cols')), may hold values from -6 to 6
Outputs:
- hidden: bfloat16 [65536, 256], P(('rows', 'cols'))
- feature_grad: bfloat16 [65536, 256], P(('cols', 'rows'))
- weight_grad: float32 [256, 256], P('rows', 'cols')
Inputs may be any that keep to these rules, and one draw needn't show every extreme that they name: Device (r, c) holds tile_count[r, c] live tiles in its first slots; tiles may share a position and then add. Some device holds 768 live tiles in every draw.
All inputs are finite; a program needn't handle non-finite values.
Results may differ from a plain program's by a relative error of at most 0.007.
Values may be sent and summed in bfloat16 or wider, within the bound.
No kernel may reach another device: no remote copies, remote signals or barrier semaphores. Data moves between devices by JAX's collectives and lax.ppermute only.
A program may use at most 128 MiB of HBM per device.

v0:
```python
import math

import jax
import jax.numpy as jnp
from jax import lax
from jax.sharding import PartitionSpec as P

TB = 64


def block_product(values, rows_index, cols_index, count, dense, out_blocks, transposed):
    ntiles = values.shape[0]
    tile = values.shape[1]
    feat = dense.shape[1]
    group = math.gcd(ntiles, 128)
    dense3 = dense.reshape(-1, tile, feat)

    def step(turn, acc):
        start = turn * group
        block_values = lax.dynamic_slice_in_dim(values, start, group, 0)
        block_rows = lax.dynamic_slice_in_dim(rows_index, start, group, 0)
        block_cols = lax.dynamic_slice_in_dim(cols_index, start, group, 0)
        live = start + jnp.arange(group, dtype=jnp.int32) < count
        if transposed:
            source = dense3[block_rows]
            prod = jnp.einsum(
                "kij,kif->kjf", block_values, source, preferred_element_type=jnp.float32
            )
            target = block_cols
        else:
            source = dense3[block_cols]
            prod = jnp.einsum(
                "kij,kjf->kif", block_values, source, preferred_element_type=jnp.float32
            )
            target = block_rows
        prod = jnp.where(live[:, None, None], prod, jnp.float32(0.0))
        return acc.at[target].add(prod)

    turns = (count + group - 1) // group
    acc = lax.fori_loop(0, turns, step, jnp.zeros((out_blocks, tile, feat), jnp.float32))
    return acc.reshape(out_blocks * tile, feat)


def body(features, weight, tile_values, tile_rows, tile_cols, tile_count, out_grad):
    values = tile_values[0, 0].reshape(tile_values.shape[2], TB, TB)
    rows_index = tile_rows[0, 0]
    cols_index = tile_cols[0, 0]
    count = tile_count[0, 0]
    node_dev = features.shape[0]
    src_nodes = node_dev * lax.axis_size("rows")
    dst_nodes = out_grad.shape[0] * lax.axis_size("cols")
    projected = jnp.dot(
        lax.all_gather(features, "rows", axis=0, tiled=True),
        weight,
        preferred_element_type=jnp.float32,
    ).astype(jnp.bfloat16)
    messages = block_product(
        values, rows_index, cols_index, count, projected, dst_nodes // TB, False
    )
    summed = lax.psum_scatter(messages, "cols", scatter_dimension=0, tiled=True)
    sig = jax.nn.sigmoid(summed)
    hidden = (summed * sig).astype(jnp.bfloat16)
    slope = (out_grad.astype(jnp.float32) * sig * (1.0 + summed * (1.0 - sig))).astype(jnp.bfloat16)
    slope_full = lax.all_gather(slope, "cols", axis=0, tiled=True)
    back_terms = block_product(
        values, rows_index, cols_index, count, slope_full, src_nodes // TB, True
    )
    back_all = lax.psum(back_terms, "rows").astype(jnp.bfloat16)
    back = lax.dynamic_slice_in_dim(back_all, lax.axis_index("rows") * node_dev, node_dev, 0)
    feature_grad = lax.dot_general(
        back, weight, (((1,), (1,)), ((), ())), preferred_element_type=jnp.float32
    )
    weight_part = lax.dot_general(
        features, back, (((0,), (0,)), ((), ())), preferred_element_type=jnp.float32
    )
    weight_band = lax.psum_scatter(weight_part, "rows", scatter_dimension=0, tiled=True)
    weight_grad = lax.psum_scatter(weight_band, "cols", scatter_dimension=1, tiled=True)
    return (hidden, feature_grad.astype(jnp.bfloat16), weight_grad)


def solution(mesh):
    return jax.shard_map(
        body,
        mesh=mesh,
        in_specs=(
            P(("cols", "rows"), None),
            P(),
            P("rows", "cols", None, None),
            P("rows", "cols", None),
            P("rows", "cols", None),
            P("rows", "cols"),
            P(("rows", "cols"), None),
        ),
        out_specs=(P(("rows", "cols"), None), P(("cols", "rows"), None), P("rows", "cols")),
        check_vma=False,
    )
```

profile of v0, /device:TPU:32, one launch (start us, length us, event | category | flops | bytes accessed | tf_op | source)
XLA Modules:
  0.0 968.7 jit_solution(16615003588001864158)
XLA Ops:
  9.3 8.6 copy.16
  18.0 53.3 %all-gather.3.cloned.1.call-done = bf16[4096,256]{1,0:T(8,128)(2,1)} async-done(((bf16[256,256]{1,0:T(8,128)(2,1)}), bf16[4096,256]{1,0:T(8,128)(2,1)}) %all-gather.3.cloned.1.call-update) | async-done | bytes 2097168 | tf_op jit(solution)/shard_map/all_gather | solution.py:53
  71.2 2.3 convolution_convert_fusion
  73.5 2.5 broadcast.35.clone
  76.1 84.6 %while.20 = (s32[]{:T(128)}, f32[64,64,256]{2,1,0:T(8,128)}, s32[]{:T(128)}, s32[768]{0:T(1024)S(1)}, s32[]{:T(128)}, /*index=5*/bf16[768,64,64]{0,2,1:T(8,128)(...) while((s32[]{:T(128)}, f32[64,64,256]{2,1,0:T(8,128)}, ...), condition=%wide.region_2.3_spmd, body=%wide.region_0.2_spmd.sunk | while | flops 272631808 | bytes 51388344 | solution.py:40
  76.8 1.3 constant_dynamic-slice_fusion.4
  78.1 3.7 copy.26
  81.9 2.8 gather_fusion
  84.7 7.3 broadcast_select_fusion.4
  91.9 26.5 %scatter_fusion = f32[64,64,256]{2,1,0:T(8,128)} fusion(f32[64,64,256]{2,1,0:T(8,128)} %get-tuple-element.299, s32[128]{0:T(128)S(1)} %get-tuple-element.274, f32[128,64,256]{2,1,0:T(8,128)} %broadcast_select_fusion.4), kind=kCustom, calls=%fused_computation.2.clone.1 | custom fusion | flops 2097152 | bytes 25166336 | tf_op jit(solution)/shard_map/while/body/scatter-add | solution.py:37
  120.4 3.7 copy.26
  124.2 2.8 gather_fusion
  127.0 7.3 broadcast_select_fusion.4
  134.2 26.5 %scatter_fusion = f32[64,64,256]{2,1,0:T(8,128)} fusion(f32[64,64,256]{2,1,0:T(8,128)} %get-tuple-element.299, s32[128]{0:T(128)S(1)} %get-tuple-element.274, f32[128,64,256]{2,1,0:T(8,128)} %broadcast_select_fusion.4), kind=kCustom, calls=%fused_computation.2.clone.1 | custom fusion | flops 2097152 | bytes 25166336 | tf_op jit(solution)/shard_map/while/body/scatter-add | solution.py:37
  160.8 234.6 %reduce-scatter.6.cloned.1.call-done = f32[256,256]{1,0:T(8,128)} async-done(((f32[4096,256]{1,0:T(8,128)}), f32[256,256]{1,0:T(8,128)}) %reduce-scatter.6.cloned.1.call-update) | async-done | bytes 262160 | tf_op jit(solution)/shard_map/reduce_scatter | solution.py:60
  395.4 1.8 multiply_convert_fusion
  397.2 35.8 %all-gather.5.cloned.1.call-done = bf16[4096,256]{1,0:T(8,128)(2,1)} async-done(((bf16[256,256]{1,0:T(8,128)(2,1)}), bf16[4096,256]{1,0:T(8,128)(2,1)}) %all-gather.5.cloned.1.call-update) | async-done | bytes 2097168 | tf_op jit(solution)/shard_map/all_gather | solution.py:64
  433.0 2.5 broadcast.35
  435.6 86.3 %while.21 = (s32[]{:T(128)}, f32[64,64,256]{2,1,0:T(8,128)}, s32[]{:T(128)}, s32[768]{0:T(1024)S(1)}, s32[]{:T(128)}, /*index=5*/bf16[768,64,64]{0,2,1:T(8,128)(...) while((s32[]{:T(128)}, f32[64,64,256]{2,1,0:T(8,128)}, ...), condition=%wide.region_6.7_spmd, body=%wide.region_4.6_spmd.sunk | while | flops 272631808 | bytes 51388344 | solution.py:40
  437.6 4.5 copy.27
  442.1 2.8 gather_fusion.1
  444.8 7.3 broadcast_select_fusion.5
  452.1 26.6 %scatter_fusion.1 = f32[64,64,256]{2,1,0:T(8,128)} fusion(f32[64,64,256]{2,1,0:T(8,128)} %get-tuple-element.335, s32[128]{0:T(128)S(1)} %get-tuple-element.284, f32[128,64,256]{2,1,0:T(8,128)} %broadcast_select_fusion.5), kind=kCustom, calls=%fused_computation.3.clone.1 | custom fusion | flops 2097152 | bytes 25166336 | tf_op jit(solution)/shard_map/while/body/scatter-add | solution.py:37
  480.8 4.5 copy.27
  485.2 2.8 gather_fusion.1
  488.0 7.3 broadcast_select_fusion.5
  495.3 26.6 %scatter_fusion.1 = f32[64,64,256]{2,1,0:T(8,128)} fusion(f32[64,64,256]{2,1,0:T(8,128)} %get-tuple-element.335, s32[128]{0:T(128)S(1)} %get-tuple-element.284, f32[128,64,256]{2,1,0:T(8,128)} %broadcast_select_fusion.5), kind=kCustom, calls=%fused_computation.3.clone.1 | custom fusion | flops 2097152 | bytes 25166336 | tf_op jit(solution)/shard_map/while/body/scatter-add | solution.py:37
  521.8 259.6 %all-reduce.1 = bf16[4096,256]{1,0:T(8,128)(2,1)S(1)} all-reduce(f32[4096,256]{1,0:T(8,128)} %bitcast.26), channel_id=1, replica_groups=mesh['rows'=16,'cols'=16] {'rows'}, use_global_device_ids=true, to_apply=%region_7.8 | all-reduce | flops 1048576 | bytes 6291456 | tf_op jit(solution)/shard_map/psum | solution.py:68
  782.6 115.8 %reduce-scatter.10.cloned.1.call-done = f32[16,256]{1,0:T(8,128)} async-done(((f32[256,256]{1,0:T(8,128)}), f32[16,256]{1,0:T(8,128)}) %reduce-scatter.10.cloned.1.call-update) | async-done | bytes 16400
  898.4 1.4 copy.21
  900.8 60.0 %reduce-scatter.8.cloned.1.call-done = f32[16,16]{0,1:T(8,128)} async-done(((f32[16,256]{0,1:T(8,128)}), f32[16,16]{0,1:T(8,128)}) %reduce-scatter.8.cloned.1.call-update) | async-done | bytes 1040 | tf_op jit(solution)/shard_map/reduce_scatter | solution.py:77
  960.8 1.4 copy.19
  (40 shorter events, 10.5 us)
Async XLA Ops:
  7.2 64.1 %copy-start = (bf16[256,256]{1,0:T(8,128)(2,1)S(1)}, bf16[256,256]{1,0:T(8,128)(2,1)}, u32[]{:S(2)}) copy-start(bf16[256,256]{1,0:T(8,128)(2,1)} %param.12) | copy-start | bytes 393220
  7.2 64.1 %all-gather.3.cloned.1.call-start = ((), (), s32[]{:S(2)}) async-start(), calls=%async_computation.3 | async-start | bytes 2228224 | tf_op jit(solution)/shard_map/all_gather | solution.py:53
  7.9 387.5 %reduce-scatter.6.cloned.1.call-start = ((), (), s32[]{:S(2)}) async-start(), calls=%async_computation.4 | async-start | bytes 4456448 | tf_op jit(solution)/shard_map/reduce_scatter | solution.py:60
  9.3 8.6 copy-start.4
  160.7 234.7 %copy-start.3 = (bf16[256,256]{1,0:T(8,128)(2,1)S(1)}, bf16[256,256]{1,0:T(8,128)(2,1)}, u32[]{:S(2)}) copy-start(bf16[256,256]{1,0:T(8,128)(2,1)} %param.17) | copy-start | bytes 393220
  160.7 272.3 %all-gather.5.cloned.1.call-start = ((), (), s32[]{:S(2)}) async-start(), calls=%async_computation.5 | async-start | bytes 2228224 | tf_op jit(solution)/shard_map/all_gather | solution.py:64
  397.2 501.2 %reduce-scatter.10.cloned.1.call-start = ((), (), s32[]{:S(2)}) async-start(), calls=%async_computation.7 | async-start | bytes 278528
  433.0 2.5 copy-start.1
  521.8 259.6 %copy-start.2 = (bf16[256,256]{1,0:T(8,128)(2,1)S(1)}, bf16[256,256]{1,0:T(8,128)(2,1)}, u32[]{:S(2)}) copy-start(bf16[256,256]{1,0:T(8,128)(2,1)} %param.11) | copy-start | bytes 393220
  782.5 178.3 %reduce-scatter.8.cloned.1.call-start = ((), (), s32[]{:S(2)}) async-start(), calls=%async_computation.6 | async-start | bytes 139264 | tf_op jit(solution)/shard_map/reduce_scatter | solution.py:77
Sparse Core Ops, SparseCore 0:
  10.4 60.7 all-gather.2
  160.8 234.5 reduce-scatter.5
  397.8 35.1 all-gather.4
  782.7 115.7 reduce-scatter.9
  900.9 59.8 reduce-scatter.7
where the time goes:
time: 985 us; the launch traced here: 969 us
  waiting for transfers between devices  500 us (51%)
  blocking collectives  260 us (26%)
  other arithmetic  111 us (11%)
  local copies, waits for them, and re-layouts  50.1 us (5%)
  matrix products  32.5 us (3%)
  between operations  14.5 us (1%)
    psum x1, blocking collectives, body(): back_all = lax.psum(back_terms, 'rows').astype(jnp.bfloat16)  260 us
    reduce_scatter x1, waiting for transfers between devices, body(): summed = lax.psum_scatter(messages, 'cols', scatter_dimension=0, tiled=True)  235 us
    unnamed x6, waiting for transfers between devices  117 us
    scatter-add x4, other arithmetic, step(): return acc.at[target].add(prod)  106 us
    reduce_scatter x1, waiting for transfers between devices, body(): lax.psum_scatter(weight_band, 'cols', scatter_dimension=1, tiled=True)  60 us
    all_gather x1, waiting for transfers between devices, body(): lax.all_gather(features, 'rows', axis=0, tiled=True)  53.3 us
    all_gather x1, waiting for transfers between devices, body(): slope_full = lax.all_gather(slope, 'cols', axis=0, tiled=True)  35.8 us
    dynamic_slice x8, local copies, waits for them, and re-layouts, step(): block_values = lax.dynamic_slice_in_dim(values, start, group, 0)  21.6 us
  transfers between devices with their start and end apart: 5, of which 5 were waited for; matrix products, arithmetic and copies ran while one was open for 1% of the time, Pallas kernels for 0%

commit v1 on v0

v1 whole, which is shorter than its diff:
```python
import functools
import jax
import jax.numpy as jnp
from jax import lax
from jax.experimental import pallas as pl
from jax.experimental.pallas import tpu as pltpu
from jax.sharding import PartitionSpec as P

TB = 64
GROUP = 16
PAIRS = TB // 2


def build_kernel(blocks, tiles, slab, count_ref, rows_ref, cols_ref, vals_ref, out_ref,
                 dense, sums, lay, slot_of, place_of, used, sem):
    turn = pl.program_id(0)
    count = count_ref[0]
    spare = blocks * blocks

    @pl.when(turn == 0)
    def _():
        def clear(i, carry):
            dense[pl.ds(pl.multiple_of(i * TB, TB), TB), :] = jnp.zeros((TB, dense.shape[1]), dense.dtype)
            for j in range(blocks):
                slot_of[i * blocks + j] = -1
            return carry
        lax.fori_loop(0, blocks, clear, 0)

        def unplace(i, carry):
            for j in range(GROUP):
                place_of[i * GROUP + j] = spare
            return carry
        lax.fori_loop(0, tiles // GROUP, unplace, 0)
        slot_of[spare] = tiles
        used[0] = 0

    def gather(g, carry):
        base = turn * slab + g * GROUP

        @pl.when(base < count)
        def _():
            for m in range(PAIRS):
                lay[m * GROUP:(m + 1) * GROUP, :] = vals_ref[
                    pl.ds(pl.multiple_of(g * GROUP, GROUP), GROUP), m * 128:(m + 1) * 128
                ].astype(jnp.float32)
            top = used[0]
            for k in range(GROUP):
                index = base + k
                place = jnp.where(index < count, rows_ref[index] * blocks + cols_ref[index], spare)
                slot = slot_of[place]
                fresh = slot < 0
                slot = jnp.where(fresh, top, slot)
                slot_of[place] = slot

                @pl.when(fresh)
                def _():
                    place_of[slot] = place
                top = jnp.where(fresh, top + 1, top)
                tile = lay[pl.ds(k, PAIRS, stride=GROUP), :]
                sums[slot] = tile + jnp.where(fresh, 0.0, sums[slot])
            used[0] = top
        return carry

    lax.fori_loop(0, slab // GROUP, gather, 0)

    @pl.when(turn == pl.num_programs(0) - 1)
    def _():
        lane_half = lax.broadcasted_iota(jnp.int32, (PAIRS, 128), 1) // TB

        def put(i, carry):
            for k in range(8):
                slot = i * 8 + k
                place = place_of[slot]
                row = place // blocks
                col = place % blocks
                half = col % 2
                tile = sums[slot]
                turned = pltpu.roll(tile, TB, 1)
                even = half == 0
                mine = lane_half == half
                lanes = pl.ds(pl.multiple_of((col // 2) * 128, 128), 128)
                for odd in range(2):
                    here = (pl.ds(pl.multiple_of(row * TB + odd * PAIRS, PAIRS), PAIRS), lanes)
                    if odd:
                        new = jnp.where(even, turned, tile)
                    else:
                        new = jnp.where(even, tile, turned)
                    old = dense[here].astype(jnp.float32)
                    dense[here] = jnp.where(mine, new, old).astype(dense.dtype)
            return carry

        lax.fori_loop(0, (used[0] + 7) // 8, put, 0)
        copy = pltpu.make_async_copy(dense.at[pl.ds(0, blocks * TB)], out_ref, sem)
        copy.start()
        copy.wait()


def build_dense(values, rows, cols, count, blocks, slab=128):
    tiles = values.shape[0]
    n = blocks * TB
    return pl.pallas_call(
        functools.partial(build_kernel, blocks, tiles, slab),
        grid=(tiles // slab,),
        in_specs=[
            pl.BlockSpec(memory_space=pltpu.SMEM),
            pl.BlockSpec(memory_space=pltpu.SMEM),
            pl.BlockSpec(memory_space=pltpu.SMEM),
            pl.BlockSpec((slab, TB * TB), lambda i: (i, 0)),
        ],
        out_specs=pl.BlockSpec(memory_space=pl.ANY),
        out_shape=jax.ShapeDtypeStruct((n, n), jnp.bfloat16),
        scratch_shapes=[
            pltpu.VMEM((n + TB, n), jnp.bfloat16),
            pltpu.VMEM((tiles + 1, PAIRS, 128), jnp.float32),
            pltpu.VMEM((GROUP * PAIRS, 128), jnp.float32),
            pltpu.SMEM((blocks * blocks + 1,), jnp.int32),
            pltpu.SMEM((tiles,), jnp.int32),
            pltpu.SMEM((1,), jnp.int32),
            pltpu.SemaphoreType.DMA,
        ],
        compiler_params=pltpu.CompilerParams(vmem_limit_bytes=56 * 1024 * 1024),
        cost_estimate=pl.CostEstimate(flops=0, bytes_accessed=64 * 1024 * 1024, transcendentals=0),
        name="build_dense",
    )(count, rows, cols, values)


def rows_shift(dz, dy):
    return [(z * 4 + y, (z + dz) % 4 * 4 + (y + dy) % 4) for z in range(4) for y in range(4)]


def cols_shift(dz, dx, dc):
    return [
        (z * 8 + x * 2 + c, (z + dz) % 2 * 8 + (x + dx) % 4 * 2 + (c + dc) % 2)
        for z in range(2) for x in range(4) for c in range(2)
    ]


def f32(x):
    return x.astype(jnp.float32)


def bf16(x):
    return x.astype(jnp.bfloat16)


def mix():
    nodes = lax.broadcasted_iota(jnp.int32, (256, 256), 0)
    natural = lax.broadcasted_iota(jnp.int32, (256, 256), 1)
    inner = nodes % TB
    source = nodes // TB * TB + inner % PAIRS * 2 + inner // PAIRS
    return bf16(source == natural)


def body(features, weight, tile_values, tile_rows, tile_cols, tile_count, out_grad):
    me_r = lax.axis_index("rows")
    me_c = lax.axis_index("cols")
    own = tile_rows[0, 0] // 4
    slot_r = (own % 2 - me_c % 2) % 2 * 8 + (own // 2 % 4 - me_c // 2 % 4) % 4 * 2 + (own // 8 - me_c // 8) % 2
    rows = slot_r * 4 + tile_rows[0, 0] % 4
    own = tile_cols[0, 0] // 4
    slot_c = (own % 4 - me_r % 4) % 4 * 4 + (own // 4 - me_r // 4) % 4
    cols = slot_c * 4 + tile_cols[0, 0] % 4

    with jax.named_scope("gather_features"):
        block = jnp.concatenate(
            [features]
            + [lax.ppermute(features, "rows", rows_shift(-dz, 0)) for dz in (1, 2, 3)], 0)
        sources = jnp.concatenate(
            [block] + [lax.ppermute(block, "rows", rows_shift(0, -dy)) for dy in (1, 2, 3)], 0)
    with jax.named_scope("build"):
        dense = build_dense(tile_values[0, 0], rows, cols, tile_count[0], 64)
    with jax.named_scope("project"):
        projected = bf16(jnp.dot(sources, weight, preferred_element_type=jnp.float32))
    with jax.named_scope("forward"):
        messages = bf16(jnp.dot(dense, projected, preferred_element_type=jnp.float32))
    with jax.named_scope("reduce_cols"):
        got = lax.ppermute(messages[2048:], "cols", cols_shift(0, 0, 1))
        part = f32(messages[:2048]) + f32(got)
        sent = bf16(part[512:])
        got = [lax.ppermute(sent[512 * (d - 1):512 * d], "cols", cols_shift(0, d, 0)) for d in (1, 2, 3)]
        part = part[:512] + f32(got[0]) + f32(got[1]) + f32(got[2])
        got = lax.ppermute(bf16(part[256:]), "cols", cols_shift(1, 0, 0))
        summed = part[:256] + f32(got)
    with jax.named_scope("activate"):
        order = mix()
        grad = jnp.dot(order, out_grad, preferred_element_type=jnp.float32)
        sig = jax.nn.sigmoid(summed)
        hidden = bf16(summed * sig)
        slope = bf16(grad * sig * (1.0 + summed * (1.0 - sig)))
        hidden = bf16(lax.dot_general(order, hidden, (((0,), (0,)), ((), ())), preferred_element_type=jnp.float32))
    with jax.named_scope("gather_slope"):
        block = jnp.concatenate([slope, lax.ppermute(slope, "cols", cols_shift(1, 0, 0))], 0)
        block = jnp.concatenate(
            [block] + [lax.ppermute(block, "cols", cols_shift(0, -d, 0)) for d in (1, 2, 3)], 0)
        slopes = jnp.concatenate([block, lax.ppermute(block, "cols", cols_shift(0, 0, 1))], 0)
    with jax.named_scope("backward"):
        terms = bf16(lax.dot_general(dense, slopes, (((0,), (0,)), ((), ())), preferred_element_type=jnp.float32))
    with jax.named_scope("reduce_rows"):
        got = [lax.ppermute(terms[1024 * d:1024 * (d + 1)], "rows", rows_shift(0, d)) for d in (1, 2, 3)]
        part = f32(terms[:1024]) + f32(got[0]) + f32(got[1]) + f32(got[2])
        sent = bf16(part[256:])
        got = [lax.ppermute(sent[256 * (d - 1):256 * d], "rows", rows_shift(d, 0)) for d in (1, 2, 3)]
        back = bf16(part[:256] + f32(got[0]) + f32(got[1]) + f32(got[2]))
    with jax.named_scope("feature_grad"):
        feature_grad = bf16(lax.dot_general(
            back, weight, (((1,), (1,)), ((), ())), preferred_element_type=jnp.float32))
    with jax.named_scope("weight_grad"):
        share = lax.dot_general(sources, terms, (((0,), (0,)), ((), ())), preferred_element_type=jnp.float32)
        band = lax.all_to_all(share, "rows", 0, 0, tiled=True)
        band = jnp.sum(band.reshape(16, 16, 256), axis=0)
        band = band.reshape(16, 16, 16).transpose(1, 0, 2).reshape(16, 256)
        band = lax.all_to_all(band, "cols", 0, 0, tiled=True)
        weight_grad = jnp.sum(band, axis=0).reshape(16, 16)
    return hidden, feature_grad, weight_grad


def solution(mesh):
    return jax.shard_map(
        body,
        mesh=mesh,
        in_specs=(
            P(("cols", "rows"), None),
            P(),
            P("rows", "cols", None, None),
            P("rows", "cols", None),
            P("rows", "cols", None),
            P("rows", "cols"),
            P(("rows", "cols"), None),
        ),
        out_specs=(P(("rows", "cols"), None), P(("cols", "rows"), None), P("rows", "cols")),
        check_vma=False,
    )
```

time: 985 us -> 210 us (0.21); the launches traced: 969 us -> 210 us
  waiting for transfers between devices: 500 us -> 55.7 us
  blocking collectives: 260 us -> 26.1 us
  other arithmetic: 111 us -> 4.21 us
  starting transfers between devices: 0.2 us -> 45.9 us
  local copies, waits for them, and re-layouts: 50.1 us -> 10.9 us
  Pallas kernels: 0 us -> 26.3 us
  between operations: 14.5 us -> 1.8 us
    reduce_scatter x2 -> x0, waiting for transfers between devices: 295 us -> none  [the longest x1 235 us: body(): summed = lax.psum_scatter(messages, 'cols', scatter_dimension=0, tiled=True)]
    psum x1 -> x0, blocking collectives: 260 us -> none  [body(): back_all = lax.psum(back_terms, 'rows').astype(jnp.bfloat16)]
    unnamed x6 -> x0, waiting for transfers between devices: 117 us -> none
    scatter-add x4 -> x0, other arithmetic: 106 us -> none  [step(): return acc.at[target].add(prod)]
    all_gather x2 -> x0, waiting for transfers between devices: 89 us -> none  [the longest x1 53.3 us: body(): lax.all_gather(features, 'rows', axis=0, tiled=True)]
    ppermute x0 -> x22, waiting for transfers between devices: none -> 55.7 us  [the longest x3 13.9 us: body(): lax.ppermute(sent[512 * (d - 1):512 * d], 'cols', cols_shift(0, d, 0))]
    ppermute x0 -> x22, starting transfers between devices: none -> 41.2 us  [the longest x3 9.29 us: body(): lax.ppermute(features, 'rows', rows_shift(-dz, 0))]
    pallas_call x0 -> x1, Pallas kernels: none -> 26.3 us  [build_dense(): pl.pallas_call(functools.partial(build_kernel, blocks, tiles, slab), grid...]
  transfers between devices with their start and end apart: 5 -> 23, of which waited for: 5 -> 14; matrix products, arithmetic and copies ran while one was open for 1% -> 6% of each run, Pallas kernels for 0% -> 13%
where the time goes in v1:
time: 210 us
  waiting for transfers between devices  55.7 us (27%)
  starting transfers between devices  45.9 us (22%)
  matrix products  38.8 us (18%)
  Pallas kernels  26.3 us (13%)
  blocking collectives  26.1 us (12%)
  local copies, waits for them, and re-layouts  10.9 us (5%)
  other arithmetic  4.21 us (2%)
    pallas_call x1, Pallas kernels, build_dense(): pl.pallas_call(functools.partial(build_kernel, blocks, tiles, slab), grid...  26.3 us
    all_to_all x1, blocking collectives, body(): band = lax.all_to_all(share, 'rows', 0, 0, tiled=True)  26.1 us
    dot_general x1, matrix products, body(): jnp.dot(dense, projected, preferred_element_type=jnp.float32)  18.2 us
    dot_general x1, matrix products, body(): lax.dot_general(dense, slopes, (((0,), (0,)), ((), ())), preferred_elemen...  15.9 us
    ppermute x3, waiting for transfers between devices, body(): lax.ppermute(sent[512 * (d - 1):512 * d], 'cols', cols_shift(0, d, 0))  13.9 us
    ppermute x3, waiting for transfers between devices, body(): lax.ppermute(block, 'cols', cols_shift(0, -d, 0))  11.6 us
    ppermute x3, waiting for transfers between devices, body(): lax.ppermute(sent[256 * (d - 1):256 * d], 'rows', rows_shift(d, 0))  10.5 us
    ppermute x3, starting transfers between devices, body(): lax.ppermute(features, 'rows', rows_shift(-dz, 0))  9.29 us
  transfers between devices with their start and end apart: 23, of which 14 were waited for; matrix products, arithmetic and copies ran while one was open for 6% of the time, Pallas kernels for 13%

profile of v1, /device:TPU:32, one launch (start us, length us, event | category | flops | bytes accessed | tf_op | source)
XLA Modules:
  0.0 209.8 jit_solution(7552342523301086870)
XLA Ops:
  0.6 5.5 %collective-permute-start = (bf16[256,256]{1,0:T(8,128)(2,1)}, bf16[256,256]{1,0:T(8,128)(2,1)S(1)}, u32[]{:S(2)}, u32[]{:S(2)}) collective-permute-start(bf16[256,256]{1,0:T(8,128)(2,1)} %param.7), channel_id=1, source_target_pairs={{0,192},{16,208},{32,224},{48,240},{64,0},{80,16},{96,32},{112,48}... | collective-permute-start | bytes 393224 | tf_op jit(solution)/shard_map/gather_features/ppermute | solution.py:167
  6.1 1.4 collective-permute-start.1
  7.6 2.4 %collective-permute-start.2 = (bf16[256,256]{1,0:T(8,128)(2,1)}, bf16[256,256]{1,0:T(8,128)(2,1)S(1)}, u32[]{:S(2)}, u32[]{:S(2)}) collective-permute-start(bf16[256,256]{1,0:T(8,128)(2,1)} %param.7), channel_id=1, source_target_pairs={{0,64},{16,80},{32,96},{48,112},{64,128},{80,144},{96,160},{112,17... | collective-permute-start | bytes 393224 | tf_op jit(solution)/shard_map/gather_features/ppermute | solution.py:167
  9.9 1.6 constant_dynamic-update-slice_fusion.3
  13.0 6.7 %collective-permute-done.1 = bf16[256,256]{1,0:T(8,128)(2,1)S(1)} collective-permute-done((bf16[256,256]{1,0:T(8,128)(2,1)}, bf16[256,256]{1,0:T(8,128)(2,1)S(1)}, u32[]{:S(2)}, u32[]{:S(2)}) %collective-permute-start.1) | collective-permute-done | bytes 131104 | tf_op jit(solution)/shard_map/gather_features/ppermute | solution.py:167
  21.0 3.0 %collective-permute-start.3 = (bf16[1024,256]{1,0:T(8,128)(2,1)S(1)}, bf16[1024,256]{1,0:T(8,128)(2,1)S(1)}, u32[]{:S(2)}, u32[]{:S(2)}) collective-permute-start(bf16[1024,256]{1,0:T(8,128)(2,1)S(1)} %get-tuple-element.26), channel_id=1, source_target_pairs={{0,48},{16,0},{32,16},{48,32},{64,112},{80,64},{96,80},{112,96},{1... | collective-permute-start | bytes 1572872 | tf_op jit(solution)/shard_map/gather_features/ppermute | solution.py:169
  28.4 26.3 %build_dense.1 = bf16[4096,4096]{1,0:T(8,128)(2,1)} custom-call(s32[1]{0:T(128)} %bitcast.13.count_ref, s32[768]{0:T(1024)} %get-tuple-element.35.rows_ref, s32[768]{0:T(1024)} %get-tuple-element.36.cols_ref, bf16[768,4096]{1,0:T(8,128)(2,1)} %bitcast.14), custom_call_target="tpu_custom_call" | custom-call | bytes 67108864 | tf_op jit(solution)/shard_map/build/build_dense/pallas_call | solution.py:101
  57.3 18.2 %convolution_convert_fusion = bf16[4096,256]{1,0:T(8,128)(2,1)S(1)} fusion(bf16[4096,4096]{1,0:T(8,128)(2,1)} %build_dense.1, bf16[4096,256]{1,0:T(8,128)(2,1)} %constant_dynamic-update-slice_fusion.4, bf16[256,256]{1,0:T(8,128)(2,1)S(1)} %copy-done.6), kind=kOutput, calls=%fused_computation | convolution fusion | flops 9128902656 | bytes 37879808 | tf_op jit(solution)/shard_map/forward/dot_general | solution.py:175
  75.6 2.6 %collective-permute-done.6 = bf16[2048,256]{1,0:T(8,128)(2,1)S(1)} collective-permute-done((bf16[2048,256]{1,0:T(8,128)(2,1)S(1)}, bf16[2048,256]{1,0:T(8,128)(2,1)S(1)}, u32[]{:S(2)}, u32[]{:S(2)}) %collective-permute-start.6) | collective-permute-done | bytes 1048608 | tf_op jit(solution)/shard_map/reduce_cols/ppermute | solution.py:177
  78.7 5.0 %collective-permute-start.9 = (bf16[512,256]{1,0:T(8,128)(2,1)S(1)}, bf16[512,256]{1,0:T(8,128)(2,1)S(1)}, u32[]{:S(2)}, u32[]{:S(2)}) collective-permute-start(bf16[512,256]{1,0:T(8,128)(2,1)S(1)} %get-tuple-element.11), channel_id=1, source_target_pairs={{0,6},{1,7},{2,0},{3,1},{4,2},{5,3},{6,4},{7,5},{8,14},{9,15},{10,... | collective-permute-start | bytes 786440 | tf_op jit(solution)/shard_map/reduce_cols/ppermute | solution.py:180
  84.7 10.5 %collective-permute-done.9 = bf16[512,256]{1,0:T(8,128)(2,1)S(1)} collective-permute-done((bf16[512,256]{1,0:T(8,128)(2,1)S(1)}, bf16[512,256]{1,0:T(8,128)(2,1)S(1)}, u32[]{:S(2)}, u32[]{:S(2)}) %collective-permute-start.9) | collective-permute-done | bytes 262176 | tf_op jit(solution)/shard_map/reduce_cols/ppermute | solution.py:180
  95.2 3.4 %collective-permute-done.7 = bf16[512,256]{1,0:T(8,128)(2,1)S(1)} collective-permute-done((bf16[512,256]{1,0:T(8,128)(2,1)S(1)}, bf16[512,256]{1,0:T(8,128)(2,1)S(1)}, u32[]{:S(2)}, u32[]{:S(2)}) %collective-permute-start.7) | collective-permute-done | bytes 262176 | tf_op jit(solution)/shard_map/reduce_cols/ppermute | solution.py:180
  98.8 6.9 %collective-permute-start.10 = (bf16[256,256]{1,0:T(8,128)(2,1)S(1)}, bf16[256,256]{1,0:T(8,128)(2,1)S(1)}, u32[]{:S(2)}, u32[]{:S(2)}) collective-permute-start(bf16[256,256]{1,0:T(8,128)(2,1)S(1)} %slice.115), channel_id=1, source_target_pairs={{0,8},{1,9},{2,10},{3,11},{4,12},{5,13},{6,14},{7,15},{8,0},{9,1},... | collective-permute-start | bytes 393224 | tf_op jit(solution)/shard_map/reduce_cols/ppermute | solution.py:182
  105.7 3.6 %collective-permute-done.10 = bf16[256,256]{1,0:T(8,128)(2,1)S(1)} collective-permute-done((bf16[256,256]{1,0:T(8,128)(2,1)S(1)}, bf16[256,256]{1,0:T(8,128)(2,1)S(1)}, u32[]{:S(2)}, u32[]{:S(2)}) %collective-permute-start.10) | collective-permute-done | bytes 131104 | tf_op jit(solution)/shard_map/reduce_cols/ppermute | solution.py:182
  109.8 1.8 collective-permute-start.11
  111.6 3.2 %collective-permute-done.11 = bf16[256,256]{1,0:T(8,128)(2,1)S(1)} collective-permute-done((bf16[256,256]{1,0:T(8,128)(2,1)S(1)}, bf16[256,256]{1,0:T(8,128)(2,1)S(1)}, u32[]{:S(2)}, u32[]{:S(2)}) %collective-permute-start.11) | collective-permute-done | bytes 131104 | tf_op jit(solution)/shard_map/gather_slope/ppermute | solution.py:192
  115.5 1.5 collective-permute-start.14
  117.1 7.2 %collective-permute-done.12 = bf16[512,256]{1,0:T(8,128)(2,1)S(1)} collective-permute-done((bf16[512,256]{1,0:T(8,128)(2,1)S(1)}, bf16[512,256]{1,0:T(8,128)(2,1)S(1)}, u32[]{:S(2)}, u32[]{:S(2)}) %collective-permute-start.12) | collective-permute-done | bytes 262176 | tf_op jit(solution)/shard_map/gather_slope/ppermute | solution.py:194
  124.3 1.7 collective-permute-done.13
  126.1 2.7 %collective-permute-done.14 = bf16[512,256]{1,0:T(8,128)(2,1)S(1)} collective-permute-done((bf16[512,256]{1,0:T(8,128)(2,1)S(1)}, bf16[512,256]{1,0:T(8,128)(2,1)S(1)}, u32[]{:S(2)}, u32[]{:S(2)}) %collective-permute-start.14) | collective-permute-done | bytes 262176 | tf_op jit(solution)/shard_map/gather_slope/ppermute | solution.py:194
  128.9 2.6 %collective-permute-done.15 = bf16[2048,256]{1,0:T(8,128)(2,1)S(1)} collective-permute-done((bf16[2048,256]{1,0:T(8,128)(2,1)S(1)}, bf16[2048,256]{1,0:T(8,128)(2,1)S(1)}, u32[]{:S(2)}, u32[]{:S(2)}) %collective-permute-start.15) | collective-permute-done | bytes 1048608 | tf_op jit(solution)/shard_map/gather_slope/ppermute | solution.py:195
  131.6 15.9 %convolution_convert_fusion.2 = bf16[4096,256]{1,0:T(8,128)(2,1)S(1)} fusion(bf16[4096,4096]{1,0:T(8,128)(2,1)} %build_dense.1, bf16[4096,256]{1,0:T(8,128)(2,1)S(1)} %constant_dynamic-update-slice_fusion.16), kind=kOutput, calls=%fused_computation.2 | convolution fusion | flops 8590983168 | bytes 37748736 | tf_op jit(solution)/shard_map/backward/dot_general | solution.py:197
  147.5 1.2 fusion.49
  148.7 4.0 %collective-permute-start.18 = (bf16[1024,256]{1,0:T(8,128)(2,1)}, bf16[1024,256]{1,0:T(8,128)(2,1)S(1)}, u32[]{:S(2)}, u32[]{:S(2)}) collective-permute-start(bf16[1024,256]{1,0:T(8,128)(2,1)} %get-tuple-element.8), channel_id=1, source_target_pairs={{0,48},{16,0},{32,16},{48,32},{64,112},{80,64},{96,80},{112,96},{1... | collective-permute-start | bytes 1572872 | tf_op jit(solution)/shard_map/reduce_rows/ppermute | solution.py:199
  153.6 2.3 %fusion.52 = f32[256,256]{1,0:T(8,128)S(1)} fusion(bf16[4096,256]{1,0:T(8,128)(2,1)} %constant_dynamic-update-slice_fusion.4, bf16[4096,256]{1,0:T(8,128)(2,1)S(1)} %convolution_convert_fusion.2), kind=kOutput, calls=%fused_computation.146 | convolution fusion | flops 536870912 | bytes 4456448 | tf_op jit(solution)/shard_map/weight_grad/dot_general | solution.py:208
  155.9 26.1 %all_to_all.19 = f32[16,16,256]{2,1,0:T(8,128)S(1)} all-to-all(f32[16,16,256]{2,1,0:T(8,128)S(1)} %bitcast.16), channel_id=1, replica_groups=mesh['rows'=16,'cols'=16] {'rows'}, dimensions={0} | all-to-all | bytes 524288 | tf_op jit(solution)/shard_map/weight_grad/all_to_all | solution.py:209
  182.9 4.7 %all-to-all-start.1 = ((f32[16,1,256]{2,1,0:T(1,128)}), f32[16,1,256]{2,1,0:T(1,128)S(1)}, u32[]{:S(2)}, u32[]{:S(2)}) async-start(f32[16,1,256]{2,1,0:T(1,128)} %all_to_all.16), calls=%async_computation.1 | async-start | bytes 32768 | tf_op jit(solution)/shard_map/weight_grad/all_to_all | solution.py:212
  189.3 1.6 fusion.48
  191.1 5.4 %collective-permute-start.20 = (bf16[256,256]{1,0:T(8,128)(2,1)S(1)}, bf16[256,256]{1,0:T(8,128)(2,1)S(1)}, u32[]{:S(2)}, u32[]{:S(2)}) collective-permute-start(bf16[256,256]{1,0:T(8,128)(2,1)S(1)} %get-tuple-element.15), channel_id=1, source_target_pairs={{0,128},{16,144},{32,160},{48,176},{64,192},{80,208},{96,224},{112... | collective-permute-start | bytes 393224 | tf_op jit(solution)/shard_map/reduce_rows/ppermute | solution.py:202
  198.4 2.0 collective-permute-done.21
  200.4 6.1 %collective-permute-done.20 = bf16[256,256]{1,0:T(8,128)(2,1)S(1)} collective-permute-done((bf16[256,256]{1,0:T(8,128)(2,1)S(1)}, bf16[256,256]{1,0:T(8,128)(2,1)S(1)}, u32[]{:S(2)}, u32[]{:S(2)}) %collective-permute-start.20) | collective-permute-done | bytes 131104 | tf_op jit(solution)/shard_map/reduce_rows/ppermute | solution.py:202
  206.5 2.4 %collective-permute-done.19 = bf16[256,256]{1,0:T(8,128)(2,1)S(1)} collective-permute-done((bf16[256,256]{1,0:T(8,128)(2,1)S(1)}, bf16[256,256]{1,0:T(8,128)(2,1)S(1)}, u32[]{:S(2)}, u32[]{:S(2)}) %collective-permute-start.19) | collective-permute-done | bytes 131104 | tf_op jit(solution)/shard_map/reduce_rows/ppermute | solution.py:202
  (99 shorter events, 18.2 us)
Async XLA Ops:
  0.6 108.7 %copy-start = (bf16[256,256]{1,0:T(8,128)(2,1)S(1)}, bf16[256,256]{1,0:T(8,128)(2,1)}, u32[]{:S(2)}) copy-start(bf16[256,256]{1,0:T(8,128)(2,1)} %param.13) | copy-start | bytes 393220
  0.6 11.7 %collective-permute-start = (bf16[256,256]{1,0:T(8,128)(2,1)}, bf16[256,256]{1,0:T(8,128)(2,1)S(1)}, u32[]{:S(2)}, u32[]{:S(2)}) collective-permute-start(bf16[256,256]{1,0:T(8,128)(2,1)} %param.7), channel_id=1, source_target_pairs={{0,192},{16,208},{32,224},{48,240},{64,0},{80,16},{96,32},{112,48}... | collective-permute-start | bytes 393224 | tf_op jit(solution)/shard_map/gather_features/ppermute | solution.py:167
  6.1 13.6 %collective-permute-start.1 = (bf16[256,256]{1,0:T(8,128)(2,1)}, bf16[256,256]{1,0:T(8,128)(2,1)S(1)}, u32[]{:S(2)}, u32[]{:S(2)}) collective-permute-start(bf16[256,256]{1,0:T(8,128)(2,1)} %param.7), channel_id=1, source_target_pairs={{0,128},{16,144},{32,160},{48,176},{64,192},{80,208},{96,224},{112... | collective-permute-start | bytes 393224 | tf_op jit(solution)/shard_map/gather_features/ppermute | solution.py:167
  7.6 12.8 %collective-permute-start.2 = (bf16[256,256]{1,0:T(8,128)(2,1)}, bf16[256,256]{1,0:T(8,128)(2,1)S(1)}, u32[]{:S(2)}, u32[]{:S(2)}) collective-permute-start(bf16[256,256]{1,0:T(8,128)(2,1)} %param.7), channel_id=1, source_target_pairs={{0,64},{16,80},{32,96},{48,112},{64,128},{80,144},{96,160},{112,17... | collective-permute-start | bytes 393224 | tf_op jit(solution)/shard_map/gather_features/ppermute | solution.py:167
  21.0 33.7 %collective-permute-start.3 = (bf16[1024,256]{1,0:T(8,128)(2,1)S(1)}, bf16[1024,256]{1,0:T(8,128)(2,1)S(1)}, u32[]{:S(2)}, u32[]{:S(2)}) collective-permute-start(bf16[1024,256]{1,0:T(8,128)(2,1)S(1)} %get-tuple-element.26), channel_id=1, source_target_pairs={{0,48},{16,0},{32,16},{48,32},{64,112},{80,64},{96,80},{112,96},{1... | collective-permute-start | bytes 1572872 | tf_op jit(solution)/shard_map/gather_features/ppermute | solution.py:169
  24.0 31.6 %collective-permute-start.4 = (bf16[1024,256]{1,0:T(8,128)(2,1)S(1)}, bf16[1024,256]{1,0:T(8,128)(2,1)S(1)}, u32[]{:S(2)}, u32[]{:S(2)}) collective-permute-start(bf16[1024,256]{1,0:T(8,128)(2,1)S(1)} %get-tuple-element.26), channel_id=1, source_target_pairs={{0,32},{16,48},{32,0},{48,16},{64,96},{80,112},{96,64},{112,80},{1... | collective-permute-start | bytes 1572872 | tf_op jit(solution)/shard_map/gather_features/ppermute | solution.py:169
  24.7 31.8 %collective-permute-start.5 = (bf16[1024,256]{1,0:T(8,128)(2,1)S(1)}, bf16[1024,256]{1,0:T(8,128)(2,1)S(1)}, u32[]{:S(2)}, u32[]{:S(2)}) collective-permute-start(bf16[1024,256]{1,0:T(8,128)(2,1)S(1)} %get-tuple-element.26), channel_id=1, source_target_pairs={{0,16},{16,32},{32,48},{48,0},{64,80},{80,96},{96,112},{112,64},{1... | collective-permute-start | bytes 1572872 | tf_op jit(solution)/shard_map/gather_features/ppermute | solution.py:169
  75.5 2.7 %collective-permute-start.6 = (bf16[2048,256]{1,0:T(8,128)(2,1)S(1)}, bf16[2048,256]{1,0:T(8,128)(2,1)S(1)}, u32[]{:S(2)}, u32[]{:S(2)}) collective-permute-start(bf16[2048,256]{1,0:T(8,128)(2,1)S(1)} %slice.76), channel_id=1, source_target_pairs={{0,1},{1,0},{2,3},{3,2},{4,5},{5,4},{6,7},{7,6},{8,9},{9,8},{10,11... | collective-permute-start | bytes 3145736 | tf_op jit(solution)/shard_map/reduce_cols/ppermute | solution.py:177
  78.7 16.5 %collective-permute-start.9 = (bf16[512,256]{1,0:T(8,128)(2,1)S(1)}, bf16[512,256]{1,0:T(8,128)(2,1)S(1)}, u32[]{:S(2)}, u32[]{:S(2)}) collective-permute-start(bf16[512,256]{1,0:T(8,128)(2,1)S(1)} %get-tuple-element.11), channel_id=1, source_target_pairs={{0,6},{1,7},{2,0},{3,1},{4,2},{5,3},{6,4},{7,5},{8,14},{9,15},{10,... | collective-permute-start | bytes 786440 | tf_op jit(solution)/shard_map/reduce_cols/ppermute | solution.py:180
  83.7 11.5 %collective-permute-start.8 = (bf16[512,256]{1,0:T(8,128)(2,1)S(1)}, bf16[512,256]{1,0:T(8,128)(2,1)S(1)}, u32[]{:S(2)}, u32[]{:S(2)}) collective-permute-start(bf16[512,256]{1,0:T(8,128)(2,1)S(1)} %get-tuple-element.12), channel_id=1, source_target_pairs={{0,4},{1,5},{2,6},{3,7},{4,0},{5,1},{6,2},{7,3},{8,12},{9,13},{10,... | collective-permute-start | bytes 786440 | tf_op jit(solution)/shard_map/reduce_cols/ppermute | solution.py:180
  83.7 14.9 %collective-permute-start.7 = (bf16[512,256]{1,0:T(8,128)(2,1)S(1)}, bf16[512,256]{1,0:T(8,128)(2,1)S(1)}, u32[]{:S(2)}, u32[]{:S(2)}) collective-permute-start(bf16[512,256]{1,0:T(8,128)(2,1)S(1)} %get-tuple-element.10), channel_id=1, source_target_pairs={{0,2},{1,3},{2,4},{3,5},{4,6},{5,7},{6,0},{7,1},{8,10},{9,11},{10,... | collective-permute-start | bytes 786440 | tf_op jit(solution)/shard_map/reduce_cols/ppermute | solution.py:180
  84.7 25.1 %copy-start.8 = (s32[256]{0:T(256)}, s32[256]{0:T(256)S(1)}, u32[]{:S(2)}) copy-start(s32[256]{0:T(256)S(1)} %get-tuple-element.37) | copy-start | bytes 3076
  84.7 25.1 %copy-start.10 = (s32[256]{0:T(256)}, s32[256]{0:T(256)S(1)}, u32[]{:S(2)}) copy-start(s32[256]{0:T(256)S(1)} %get-tuple-element.38) | copy-start | bytes 3076
  98.7 11.1 %copy-start.2 = (f32[512,256]{1,0:T(8,128)}, f32[512,256]{1,0:T(8,128)S(1)}, u32[]{:S(2)}) copy-start(f32[512,256]{1,0:T(8,128)S(1)} %fusion.1) | copy-start | bytes 1572868
  98.8 10.6 %collective-permute-start.10 = (bf16[256,256]{1,0:T(8,128)(2,1)S(1)}, bf16[256,256]{1,0:T(8,128)(2,1)S(1)}, u32[]{:S(2)}, u32[]{:S(2)}) collective-permute-start(bf16[256,256]{1,0:T(8,128)(2,1)S(1)} %slice.115), channel_id=1, source_target_pairs={{0,8},{1,9},{2,10},{3,11},{4,12},{5,13},{6,14},{7,15},{8,0},{9,1},... | collective-permute-start | bytes 393224 | tf_op jit(solution)/shard_map/reduce_cols/ppermute | solution.py:182
  105.7 9.2 %copy-start.18 = (pred[256]{0:T(512)(128)(4,1)}, pred[256]{0:T(512)(128)(4,1)S(1)}, u32[]{:S(2)}) copy-start(pred[256]{0:T(512)(128)(4,1)S(1)} %get-tuple-element.39) | copy-start | bytes 772
  105.7 9.2 %copy-start.20 = (pred[256]{0:T(512)(128)(4,1)}, pred[256]{0:T(512)(128)(4,1)S(1)}, u32[]{:S(2)}) copy-start(pred[256]{0:T(512)(128)(4,1)S(1)} %get-tuple-element.40) | copy-start | bytes 772
  105.7 9.2 %copy-start.12 = (s32[256]{0:T(256)}, s32[256]{0:T(256)S(1)}, u32[]{:S(2)}) copy-start(s32[256]{0:T(256)S(1)} %get-tuple-element.41) | copy-start | bytes 3076
  109.8 5.1 %collective-permute-start.11 = (bf16[256,256]{1,0:T(8,128)(2,1)S(1)}, bf16[256,256]{1,0:T(8,128)(2,1)S(1)}, u32[]{:S(2)}, u32[]{:S(2)}) collective-permute-start(bf16[256,256]{1,0:T(8,128)(2,1)S(1)} %get-tuple-element.34), channel_id=1, source_target_pairs={{0,8},{1,9},{2,10},{3,11},{4,12},{5,13},{6,14},{7,15},{8,0},{9,1},... | collective-permute-start | bytes 393224 | tf_op jit(solution)/shard_map/gather_slope/ppermute | solution.py:192
  114.9 9.3 %collective-permute-start.12 = (bf16[512,256]{1,0:T(8,128)(2,1)S(1)}, bf16[512,256]{1,0:T(8,128)(2,1)S(1)}, u32[]{:S(2)}, u32[]{:S(2)}) collective-permute-start(bf16[512,256]{1,0:T(8,128)(2,1)S(1)} %pad_maximum_fusion), channel_id=1, source_target_pairs={{0,6},{1,7},{2,0},{3,1},{4,2},{5,3},{6,4},{7,5},{8,14},{9,15},{10,... | collective-permute-start | bytes 786440 | tf_op jit(solution)/shard_map/gather_slope/ppermute | solution.py:194
  115.4 10.7 %collective-permute-start.13 = (bf16[512,256]{1,0:T(8,128)(2,1)S(1)}, bf16[512,256]{1,0:T(8,128)(2,1)S(1)}, u32[]{:S(2)}, u32[]{:S(2)}) collective-permute-start(bf16[512,256]{1,0:T(8,128)(2,1)S(1)} %pad_maximum_fusion), channel_id=1, source_target_pairs={{0,4},{1,5},{2,6},{3,7},{4,0},{5,1},{6,2},{7,3},{8,12},{9,13},{10,... | collective-permute-start | bytes 786440 | tf_op jit(solution)/shard_map/gather_slope/ppermute | solution.py:194
  115.5 13.3 %collective-permute-start.14 = (bf16[512,256]{1,0:T(8,128)(2,1)S(1)}, bf16[512,256]{1,0:T(8,128)(2,1)S(1)}, u32[]{:S(2)}, u32[]{:S(2)}) collective-permute-start(bf16[512,256]{1,0:T(8,128)(2,1)S(1)} %pad_maximum_fusion), channel_id=1, source_target_pairs={{0,2},{1,3},{2,4},{3,5},{4,6},{5,7},{6,0},{7,1},{8,10},{9,11},{10,... | collective-permute-start | bytes 786440 | tf_op jit(solution)/shard_map/gather_slope/ppermute | solution.py:194
  128.8 2.7 %collective-permute-start.15 = (bf16[2048,256]{1,0:T(8,128)(2,1)S(1)}, bf16[2048,256]{1,0:T(8,128)(2,1)S(1)}, u32[]{:S(2)}, u32[]{:S(2)}) collective-permute-start(bf16[2048,256]{1,0:T(8,128)(2,1)S(1)} %get-tuple-element.16), channel_id=1, source_target_pairs={{0,1},{1,0},{2,3},{3,2},{4,5},{5,4},{6,7},{7,6},{8,9},{9,8},{10,11... | collective-permute-start | bytes 3145736 | tf_op jit(solution)/shard_map/gather_slope/ppermute | solution.py:195
  148.7 39.0 %collective-permute-start.18 = (bf16[1024,256]{1,0:T(8,128)(2,1)}, bf16[1024,256]{1,0:T(8,128)(2,1)S(1)}, u32[]{:S(2)}, u32[]{:S(2)}) collective-permute-start(bf16[1024,256]{1,0:T(8,128)(2,1)} %get-tuple-element.8), channel_id=1, source_target_pairs={{0,48},{16,0},{32,16},{48,32},{64,112},{80,64},{96,80},{112,96},{1... | collective-permute-start | bytes 1572872 | tf_op jit(solution)/shard_map/reduce_rows/ppermute | solution.py:199
  152.7 35.0 %collective-permute-start.17 = (bf16[1024,256]{1,0:T(8,128)(2,1)}, bf16[1024,256]{1,0:T(8,128)(2,1)S(1)}, u32[]{:S(2)}, u32[]{:S(2)}) collective-permute-start(bf16[1024,256]{1,0:T(8,128)(2,1)} %get-tuple-element.9), channel_id=1, source_target_pairs={{0,32},{16,48},{32,0},{48,16},{64,96},{80,112},{96,64},{112,80},{1... | collective-permute-start | bytes 1572872 | tf_op jit(solution)/shard_map/reduce_rows/ppermute | solution.py:199
  152.7 36.6 %collective-permute-start.16 = (bf16[1024,256]{1,0:T(8,128)(2,1)}, bf16[1024,256]{1,0:T(8,128)(2,1)}, u32[]{:S(2)}, u32[]{:S(2)}) collective-permute-start(bf16[1024,256]{1,0:T(8,128)(2,1)} %get-tuple-element.7), channel_id=1, source_target_pairs={{0,16},{16,32},{32,48},{48,0},{64,80},{80,96},{96,112},{112,64},{1... | collective-permute-start | bytes 1572872 | tf_op jit(solution)/shard_map/reduce_rows/ppermute | solution.py:199
  182.9 14.8 %all-to-all-start.1 = ((f32[16,1,256]{2,1,0:T(1,128)}), f32[16,1,256]{2,1,0:T(1,128)S(1)}, u32[]{:S(2)}, u32[]{:S(2)}) async-start(f32[16,1,256]{2,1,0:T(1,128)} %all_to_all.16), calls=%async_computation.1 | async-start | bytes 32768 | tf_op jit(solution)/shard_map/weight_grad/all_to_all | solution.py:212
  190.9 18.0 %copy-start.7 = (bf16[256,256]{1,0:T(8,128)(2,1)S(1)}, bf16[256,256]{1,0:T(8,128)(2,1)}, u32[]{:S(2)}) copy-start(bf16[256,256]{1,0:T(8,128)(2,1)} %param.8) | copy-start | bytes 393220
  191.0 9.4 %collective-permute-start.21 = (bf16[256,256]{1,0:T(8,128)(2,1)S(1)}, bf16[256,256]{1,0:T(8,128)(2,1)S(1)}, u32[]{:S(2)}, u32[]{:S(2)}) collective-permute-start(bf16[256,256]{1,0:T(8,128)(2,1)S(1)} %get-tuple-element.14), channel_id=1, source_target_pairs={{0,192},{16,208},{32,224},{48,240},{64,0},{80,16},{96,32},{112,48}... | collective-permute-start | bytes 393224 | tf_op jit(solution)/shard_map/reduce_rows/ppermute | solution.py:202
  191.1 15.4 %collective-permute-start.20 = (bf16[256,256]{1,0:T(8,128)(2,1)S(1)}, bf16[256,256]{1,0:T(8,128)(2,1)S(1)}, u32[]{:S(2)}, u32[]{:S(2)}) collective-permute-start(bf16[256,256]{1,0:T(8,128)(2,1)S(1)} %get-tuple-element.15), channel_id=1, source_target_pairs={{0,128},{16,144},{32,160},{48,176},{64,192},{80,208},{96,224},{112... | collective-permute-start | bytes 393224 | tf_op jit(solution)/shard_map/reduce_rows/ppermute | solution.py:202
  196.4 13.4 %copy-start.1 = (bf16[256,256]{1,0:T(8,128)(2,1)S(1)}, bf16[256,256]{1,0:T(8,128)(2,1)}, u32[]{:S(2)}) copy-start(bf16[256,256]{1,0:T(8,128)(2,1)} %param.13) | copy-start | bytes 393220
  196.4 12.5 %collective-permute-start.19 = (bf16[256,256]{1,0:T(8,128)(2,1)S(1)}, bf16[256,256]{1,0:T(8,128)(2,1)S(1)}, u32[]{:S(2)}, u32[]{:S(2)}) collective-permute-start(bf16[256,256]{1,0:T(8,128)(2,1)S(1)} %get-tuple-element.13), channel_id=1, source_target_pairs={{0,64},{16,80},{32,96},{48,112},{64,128},{80,144},{96,160},{112,17... | collective-permute-start | bytes 393224 | tf_op jit(solution)/shard_map/reduce_rows/ppermute | solution.py:202
  (13 other events, 89.5 us)

commit v2 on v1

v2 whole, which is shorter than its diff:
```python
import functools
import jax
import jax.numpy as jnp
from jax import lax
from jax.experimental import pallas as pl
from jax.experimental.pallas import tpu as pltpu
from jax.sharding import PartitionSpec as P

TB = 64
PAIRS = TB // 2
GROUP = 16
SIDE = 64
TILES = 768
BANDS = 8
BAND = SIDE * TB // BANDS
WIDE = SIDE // 2
F = 256
UNROLL = 8
NODES = SIDE * TB
VMEM_LIMIT = 56 * 1024 * 1024


def plan_tiles(rows, cols, count):
    index = jnp.arange(TILES, dtype=jnp.int32)
    live = index < count
    pair = rows * WIDE + (cols >> 1)
    key = jnp.where(live, pair, SIDE * WIDE) * 1024 + index
    rank = jnp.sum((key[None, :] < key[:, None]).astype(jnp.int32), axis=1)
    code = index + 1024 * (pair & (BAND // TB * WIDE - 1))
    order = jnp.sum(jnp.where(rank[None, :] == index[:, None], code[None, :], 0), axis=1)
    bands = jnp.arange(BANDS + 1, dtype=jnp.int32)
    edge = bands * (BAND // TB * WIDE * 1024)
    starts = jnp.sum((key[None, :] < edge[:, None]).astype(jnp.int32), axis=1)
    return order, starts


def build_kernel(slab, order_ref, starts_ref, cols_ref, vals_ref, after_ref, dense_ref, turned_ref, lay):
    turn = pl.program_id(0)
    slabs = TILES // slab

    @pl.when(turn < slabs)
    def _():
        lane_half = lax.broadcasted_iota(jnp.int32, (PAIRS, 128), 1) >> 6

        def relay(g, carry):
            for m in range(PAIRS):
                lay[m * GROUP:(m + 1) * GROUP, :] = vals_ref[
                    pl.ds(pl.multiple_of(g * GROUP, GROUP), GROUP), m * 128:(m + 1) * 128
                ].astype(jnp.float32)
            base = turn * slab + g * GROUP
            for k in range(GROUP):
                tile = lay[pl.ds(k, PAIRS, stride=GROUP), :]
                other = pltpu.roll(tile, TB, 1)
                right = cols_ref[base + k] & 1
                mine = lane_half == right
                left = right == 0
                turned_ref[base + k, :PAIRS] = jnp.where(
                    mine, jnp.where(left, tile, other), 0.0).astype(turned_ref.dtype)
                turned_ref[base + k, PAIRS:] = jnp.where(
                    mine, jnp.where(left, other, tile), 0.0).astype(turned_ref.dtype)
            return carry

        lax.fori_loop(0, slab // GROUP, relay, 0)

    @pl.when(turn >= slabs)
    def _():
        low = starts_ref[turn - slabs]
        high = starts_ref[turn - slabs + 1]
        dense_ref[...] = jnp.zeros(dense_ref.shape, dense_ref.dtype)

        def put(i, carry):
            before, block = carry
            for k in range(UNROLL):
                spot = low + i * UNROLL + k
                code = order_ref[jnp.minimum(spot, high - 1)]
                place = code >> 10
                keep = jnp.where(place == before, 1.0, 0.0)
                add = jnp.where(spot < high, 1.0, 0.0)
                block = block * keep + turned_ref[code & 1023].astype(jnp.float32) * add
                before = place
                rows = pl.ds(pl.multiple_of((place >> 5) << 6, TB), TB)
                lanes = pl.ds(pl.multiple_of((place & 31) << 7, 128), 128)
                dense_ref[rows, lanes] = block.astype(dense_ref.dtype)
            return before, block

        none = jnp.zeros((TB, 128), jnp.float32)
        lax.fori_loop(0, (high - low + UNROLL - 1) >> 3, put, (jnp.int32(-1), none))


def build_dense(values, cols, order, starts, after, slab=256):
    slabs = TILES // slab
    return pl.pallas_call(
        functools.partial(build_kernel, slab),
        grid=(slabs + BANDS,),
        in_specs=[
            pl.BlockSpec(memory_space=pltpu.SMEM),
            pl.BlockSpec(memory_space=pltpu.SMEM),
            pl.BlockSpec(memory_space=pltpu.SMEM),
            pl.BlockSpec((slab, TB * TB), lambda i: (jnp.minimum(i, slabs - 1), 0)),
            pl.BlockSpec(memory_space=pl.ANY),
        ],
        out_specs=pl.BlockSpec((BAND, NODES), lambda i: (jnp.maximum(i - slabs, 0), 0)),
        out_shape=jax.ShapeDtypeStruct((NODES, NODES), jnp.bfloat16),
        scratch_shapes=[
            pltpu.VMEM((TILES, TB, 128), jnp.bfloat16),
            pltpu.VMEM((GROUP * PAIRS, 128), jnp.float32),
        ],
        compiler_params=pltpu.CompilerParams(vmem_limit_bytes=VMEM_LIMIT),
        cost_estimate=pl.CostEstimate(flops=0, bytes_accessed=45 * 1024 * 1024, transcendentals=0),
        name="build_dense",
    )(order, starts, cols, values, after)


def forward_kernel(after_ref, dense_ref, *refs):
    pieces, (keep_ref, send_ref), whole = refs[:-3], refs[-3:-1], refs[-1]
    turn = pl.program_id(0)

    @pl.when(turn == 0)
    def _():
        for k, piece in enumerate(pieces):
            size = piece.shape[0]
            whole[k * size:(k + 1) * size, :] = piece[...]

    total = jnp.dot(dense_ref[...], whole[...], preferred_element_type=jnp.float32)

    @pl.when(turn == 0)
    def _():
        send_ref[...] = total.astype(send_ref.dtype)

    @pl.when(turn == 1)
    def _():
        keep_ref[...] = total.astype(keep_ref.dtype)


def forward_part(dense, pieces, dx, after):
    half = NODES // 8
    out = pl.BlockSpec((half, F), lambda i: (0, 0))
    return pl.pallas_call(
        forward_kernel,
        grid=(2,),
        in_specs=[pl.BlockSpec(memory_space=pl.ANY), pl.BlockSpec((half, NODES), lambda i: (2 * dx + 1 - i, 0))]
        + [pl.BlockSpec(p.shape, lambda i: (0, 0)) for p in pieces],
        out_specs=[out, out],
        out_shape=[jax.ShapeDtypeStruct((half, F), jnp.bfloat16)] * 2,
        scratch_shapes=[pltpu.VMEM((NODES, F), jnp.bfloat16)],
        compiler_params=pltpu.CompilerParams(vmem_limit_bytes=VMEM_LIMIT),
        cost_estimate=pl.CostEstimate(
            flops=4 * half * NODES * F, bytes_accessed=11 * 1024 * 1024, transcendentals=0),
        name="forward_part",
    )(after, dense, *pieces)


def backward_kernel(after_ref, dense_ref, *refs):
    pieces, out_ref, whole = refs[:-2], refs[-2], refs[-1]

    @pl.when(pl.program_id(0) == 0)
    def _():
        for k, piece in enumerate(pieces):
            size = piece.shape[0]
            whole[k * size:(k + 1) * size, :] = piece[...]

    out_ref[...] = lax.dot_general(
        dense_ref[...], whole[...], (((0,), (0,)), ((), ())), preferred_element_type=jnp.float32
    ).astype(out_ref.dtype)


def backward_part(dense, pieces, dy, after, width=512):
    part = NODES // 4
    steps = part // width
    return pl.pallas_call(
        backward_kernel,
        grid=(steps,),
        in_specs=[pl.BlockSpec(memory_space=pl.ANY), pl.BlockSpec((NODES, width), lambda i: (0, steps * dy + i))]
        + [pl.BlockSpec(p.shape, lambda i: (0, 0)) for p in pieces],
        out_specs=pl.BlockSpec((width, F), lambda i: (i, 0)),
        out_shape=jax.ShapeDtypeStruct((part, F), jnp.bfloat16),
        scratch_shapes=[pltpu.VMEM((NODES, F), jnp.bfloat16)],
        compiler_params=pltpu.CompilerParams(vmem_limit_bytes=VMEM_LIMIT),
        cost_estimate=pl.CostEstimate(
            flops=2 * part * NODES * F, bytes_accessed=11 * 1024 * 1024, transcendentals=0),
        name="backward_part",
    )(after, dense, *pieces)


def rows_shift(dz, dy):
    return [(z * 4 + y, (z + dz) % 4 * 4 + (y + dy) % 4) for z in range(4) for y in range(4)]


def cols_shift(dz, dx, dc):
    return [
        (z * 8 + x * 2 + c, (z + dz) % 2 * 8 + (x + dx) % 4 * 2 + (c + dc) % 2)
        for z in range(2) for x in range(4) for c in range(2)
    ]


def f32(x):
    return x.astype(jnp.float32)


def bf16(x):
    return x.astype(jnp.bfloat16)


def dot(a, b, ca=1, cb=0):
    return lax.dot_general(a, b, (((ca,), (cb,)), ((), ())), preferred_element_type=jnp.float32)


def mix():
    nodes = lax.broadcasted_iota(jnp.int32, (256, 256), 0)
    natural = lax.broadcasted_iota(jnp.int32, (256, 256), 1)
    inner = nodes & (TB - 1)
    source = (nodes & ~(TB - 1)) + (inner & (PAIRS - 1)) * 2 + (inner >> 5)
    return bf16(source == natural)


def body(features, weight, tile_values, tile_rows, tile_cols, tile_count, out_grad):
    me_r = lax.axis_index("rows")
    me_c = lax.axis_index("cols")
    own = tile_rows[0, 0] >> 2
    slot_r = (((own >> 1) - (me_c >> 1)) & 3) * 4 + ((own ^ me_c) & 1) * 2 + (((own ^ me_c) >> 3) & 1)
    rows = slot_r * 4 + (tile_rows[0, 0] & 3)
    own = tile_cols[0, 0] >> 2
    slot_c = ((own - me_r) & 3) * 4 + (((own >> 2) - (me_r >> 2)) & 3)
    cols = slot_c * 4 + (tile_cols[0, 0] & 3)

    with jax.named_scope("gather_features"):
        block = jnp.concatenate(
            [features] + [lax.ppermute(features, "rows", rows_shift(-dz, 0)) for dz in (1, 2, 3)], 0)
        sources = [block] + [lax.ppermute(block, "rows", rows_shift(0, -dy)) for dy in (1, 2, 3)]
    with jax.named_scope("build"):
        order, starts = plan_tiles(rows, cols, tile_count[0, 0])
        dense = build_dense(tile_values[0, 0], cols, order, starts, block)
    parts = {}
    after = block
    for dx in (2, 1, 3, 0):
        with jax.named_scope("forward"):
            keep, send = forward_part(dense, sources, dx, after)
        with jax.named_scope("reduce_cols"):
            after = parts.get("sent", block)
            part = f32(keep) + f32(lax.ppermute(send, "cols", cols_shift(0, 0, 1)))
            if dx:
                parts["sent"] = bf16(part)
                part = f32(lax.ppermute(parts["sent"], "cols", cols_shift(0, dx, 0)))
            parts[dx] = part
    with jax.named_scope("reduce_cols"):
        part = parts[0] + parts[1] + parts[2] + parts[3]
        got = lax.ppermute(bf16(part[256:]), "cols", cols_shift(1, 0, 0))
        gathered = part[:256] + f32(got)
        high = bf16(gathered)
        low = bf16(gathered - f32(high))
        summed = dot(high, weight) + dot(low, weight)
    with jax.named_scope("activate"):
        order = mix()
        grad = dot(order, out_grad)
        sig = jax.nn.sigmoid(summed)
        slope = bf16(grad * sig * (1.0 + summed * (1.0 - sig)))
        hidden = bf16(dot(order, bf16(summed * sig), 0, 0))
    with jax.named_scope("gather_slope"):
        block = jnp.concatenate([slope, lax.ppermute(slope, "cols", cols_shift(1, 0, 0))], 0)
        slopes = []
        for dx in range(4):
            mine = lax.ppermute(block, "cols", cols_shift(0, -dx, 0)) if dx else block
            slopes += [mine, lax.ppermute(mine, "cols", cols_shift(0, 0, 1))]
    with jax.named_scope("weight_grad"):
        share = dot(high, slope, 0, 0) + dot(low, slope, 0, 0)
        band = lax.all_to_all(share, "rows", 0, 0, tiled=True)
    terms, got = {}, {}
    for dy in (2, 1, 3, 0):
        with jax.named_scope("backward"):
            terms[dy] = backward_part(dense, slopes, dy, band)
        with jax.named_scope("reduce_rows"):
            got[dy] = lax.ppermute(terms[dy], "rows", rows_shift(0, dy)) if dy else terms[dy]
    with jax.named_scope("reduce_rows"):
        part = f32(got[0]) + f32(got[1]) + f32(got[2]) + f32(got[3])
        sent = bf16(part[256:])
        got = [lax.ppermute(sent[256 * (d - 1):256 * d], "rows", rows_shift(d, 0)) for d in (1, 2, 3)]
        back = bf16(part[:256] + f32(got[0]) + f32(got[1]) + f32(got[2]))
    with jax.named_scope("feature_grad"):
        feature_grad = bf16(dot(back, weight, 1, 1))
    with jax.named_scope("weight_grad"):
        band = jnp.sum(band.reshape(16, 16, 256), axis=0)
        band = band.reshape(16, 16, 16).transpose(1, 0, 2).reshape(16, 256)
        band = lax.all_to_all(band, "cols", 0, 0, tiled=True)
        weight_grad = jnp.sum(band, axis=0).reshape(16, 16)
    return hidden, feature_grad, weight_grad


def solution(mesh):
    return jax.shard_map(
        body,
        mesh=mesh,
        in_specs=(
            P(("cols", "rows"), None),
            P(),
            P("rows", "cols", None, None),
            P("rows", "cols", None),
            P("rows", "cols", None),
            P("rows", "cols"),
            P(("rows", "cols"), None),
        ),
        out_specs=(P(("rows", "cols"), None), P(("cols", "rows"), None), P("rows", "cols")),
        check_vma=False,
    )
```

time: 210 us -> 181 us (0.86)
  Pallas kernels: 26.3 us -> 71.9 us
  matrix products: 38.8 us -> 3.62 us
  blocking collectives: 26.1 us -> 0 us
  waiting for transfers between devices: 55.7 us -> 38.2 us
  starting transfers between devices: 45.9 us -> 53.4 us
  local copies, waits for them, and re-layouts: 10.9 us -> 5.27 us
    pallas_call x1 -> x9, Pallas kernels: 26.3 us -> 71.9 us  [the longest x4 25.2 us: forward_part(): pl.pallas_call(forward_kernel, grid=(2,), in_specs=[pl.BlockSpec(memory_s...]
    dot_general x6 -> x7, matrix products: 38.8 us -> 3.62 us  [dot(): lax.dot_general(a, b, (((ca,), (cb,)), ((), ())), preferred_element_type=...]
    all_to_all x1 -> x0, blocking collectives: 26.1 us -> none  [body(): band = lax.all_to_all(share, 'rows', 0, 0, tiled=True)]
    ppermute x11 -> x17, waiting for transfers between devices: 30.9 us -> 7.56 us  [the longest x3 6.03 us: body(): part = f32(lax.ppermute(parts['sent'], 'cols', cols_shift(0, dx, 0)))]
    all_to_all x0 -> x1, waiting for transfers between devices: none -> 9.56 us  [body(): band = lax.all_to_all(share, 'rows', 0, 0, tiled=True)]
    all_to_all x0 -> x1, starting transfers between devices: none -> 7.45 us  [body(): band = lax.all_to_all(share, 'rows', 0, 0, tiled=True)]
    ppermute x1, starting transfers between devices: 6.91 us -> 1.6 us  [body(): got = lax.ppermute(bf16(part[256:]), 'cols', cols_shift(1, 0, 0))]
    ppermute x11 -> x17, starting transfers between devices: 13.1 us -> 17.9 us  [the longest x3 6.58 us: body(): part = f32(lax.ppermute(parts['sent'], 'cols', cols_shift(0, dx, 0)))]
  transfers between devices with their start and end apart: 23 -> 30, of which waited for: 14 -> 10; matrix products, arithmetic and copies ran while one was open for 6% -> 5% of each run, Pallas kernels for 13% -> 33%
where the time goes in v2:
time: 181 us; the launch traced here: 180 us
  Pallas kernels  71.9 us (40%)
  starting transfers between devices  53.4 us (30%)
  waiting for transfers between devices  38.2 us (21%)
  other arithmetic  6.15 us (3%)
  local copies, waits for them, and re-layouts  5.27 us (3%)
  matrix products  3.62 us (2%)
    pallas_call x4, Pallas kernels, forward_part(): pl.pallas_call(forward_kernel, grid=(2,), in_specs=[pl.BlockSpec(memory_s...  25.2 us
    pallas_call x4, Pallas kernels, backward_part(): pl.pallas_call(backward_kernel, grid=(steps,), in_specs=[pl.BlockSpec(mem...  25 us
    pallas_call x1, Pallas kernels, build_dense(): pl.pallas_call(functools.partial(build_kernel, slab), grid=(slabs + BANDS...  21.7 us
    all_to_all x1, waiting for transfers between devices, body(): band = lax.all_to_all(share, 'rows', 0, 0, tiled=True)  9.56 us
    ppermute x3, starting transfers between devices, body(): lax.ppermute(features, 'rows', rows_shift(-dz, 0))  9.3 us
    ppermute x3, waiting for transfers between devices, body(): lax.ppermute(sent[256 * (d - 1):256 * d], 'rows', rows_shift(d, 0))  8.3 us
    all_to_all x1, starting transfers between devices, body(): band = lax.all_to_all(share, 'rows', 0, 0, tiled=True)  7.45 us
    ppermute x3, starting transfers between devices, body(): part = f32(lax.ppermute(parts['sent'], 'cols', cols_shift(0, dx, 0)))  6.58 us
  transfers between devices with their start and end apart: 30, of which 10 were waited for; matrix products, arithmetic and copies ran while one was open for 5% of the time, Pallas kernels for 33%

profile of v2, /device:TPU:32, one launch (start us, length us, event | category | flops | bytes accessed | tf_op | source)
XLA Modules:
  0.0 180.2 jit_solution(6647983991934648220)
XLA Ops:
  0.6 6.4 %collective-permute-start.1 = (bf16[256,256]{1,0:T(8,128)(2,1)}, bf16[256,256]{1,0:T(8,128)(2,1)S(1)}, u32[]{:S(2)}, u32[]{:S(2)}) collective-permute-start(bf16[256,256]{1,0:T(8,128)(2,1)} %param.7), channel_id=1, source_target_pairs={{0,128},{16,144},{32,160},{48,176},{64,192},{80,208},{96,224},{112... | collective-permute-start | bytes 393224 | tf_op jit(solution)/shard_map/gather_features/ppermute | solution.py:228
  7.6 2.4 %collective-permute-start.2 = (bf16[256,256]{1,0:T(8,128)(2,1)}, bf16[256,256]{1,0:T(8,128)(2,1)S(1)}, u32[]{:S(2)}, u32[]{:S(2)}) collective-permute-start(bf16[256,256]{1,0:T(8,128)(2,1)} %param.7), channel_id=1, source_target_pairs={{0,64},{16,80},{32,96},{48,112},{64,128},{80,144},{96,160},{112,17... | collective-permute-start | bytes 393224 | tf_op jit(solution)/shard_map/gather_features/ppermute | solution.py:228
  13.0 5.6 %collective-permute-done = bf16[256,256]{1,0:T(8,128)(2,1)S(1)} collective-permute-done((bf16[256,256]{1,0:T(8,128)(2,1)}, bf16[256,256]{1,0:T(8,128)(2,1)S(1)}, u32[]{:S(2)}, u32[]{:S(2)}) %collective-permute-start) | collective-permute-done | bytes 131104 | tf_op jit(solution)/shard_map/gather_features/ppermute | solution.py:228
  19.1 1.7 collective-permute-start.5
  20.7 2.9 %collective-permute-start.4 = (bf16[1024,256]{1,0:T(8,128)(2,1)S(1)}, bf16[1024,256]{1,0:T(8,128)(2,1)S(1)}, u32[]{:S(2)}, u32[]{:S(2)}) collective-permute-start(bf16[1024,256]{1,0:T(8,128)(2,1)S(1)} %constant_dynamic-update-slice_fusion.after_ref.refs_0_), channel_id=1, source_target_pairs={{0,32},{16,48},{32,0},{48,16},{64,96},{80,112},{96,64},{112,80},{1... | collective-permute-start | bytes 1572872 | tf_op jit(solution)/shard_map/gather_features/ppermute | solution.py:229
  23.6 1.3 collective-permute-start.3
  27.0 21.7 %build_dense.1.dense_ref = bf16[4096,4096]{1,0:T(8,128)(2,1)} custom-call(s32[768]{0:T(1024)} %select_reduce_fusion.order_ref, s32[9]{0:T(128)} %convert_reduce_fusion.1.starts_ref, s32[768]{0:T(1024)} %copy-done.20, bf16[768,4096]{1,0:T(8,128)(2,1)} %bitcast.20, bf16[1024,256]{1,0:T(8,128)(2,1)} %copy-done.1), custom_call_target="tpu_custom_call" | custom-call | bytes 47185920 | tf_op jit(solution)/shard_map/build/build_dense/pallas_call | solution.py:92
  50.5 6.3 %forward_part.6 = (bf16[512,256]{1,0:T(8,128)(2,1)}, bf16[512,256]{1,0:T(8,128)(2,1)}) custom-call(bf16[1024,256]{1,0:T(8,128)(2,1)} %copy-done.1, bf16[4096,4096]{1,0:T(8,128)(2,1)} %build_dense.1.dense_ref, bf16[1024,256]{1,0:T(8,128)(2,1)} %copy-done.1, bf16[1024,256]{1,0:T(8,128)(2,1)} %copy-done.6, bf16[1024,256]{1,0:T(8,128)(2,1)} %copy-done.5, ...), custom_call_target="tpu_custom_call" | custom-call | flops 2147483648 | bytes 11534336 | tf_op jit(solution)/shard_map/forward/forward_part/pallas_call | solution.py:138
  56.8 6.3 %forward_part.4 = (bf16[512,256]{1,0:T(8,128)(2,1)}, bf16[512,256]{1,0:T(8,128)(2,1)}) custom-call(bf16[1024,256]{1,0:T(8,128)(2,1)} %copy-done.1, bf16[4096,4096]{1,0:T(8,128)(2,1)} %build_dense.1.dense_ref, bf16[1024,256]{1,0:T(8,128)(2,1)} %copy-done.1, bf16[1024,256]{1,0:T(8,128)(2,1)} %copy-done.6, bf16[1024,256]{1,0:T(8,128)(2,1)} %copy-done.5, ...), custom_call_target="tpu_custom_call" | custom-call | flops 2147483648 | bytes 11534336 | tf_op jit(solution)/shard_map/forward/forward_part/pallas_call | solution.py:138
  63.7 3.0 %collective-permute-start.10 = (bf16[512,256]{1,0:T(8,128)(2,1)S(1)}, bf16[512,256]{1,0:T(8,128)(2,1)S(1)}, u32[]{:S(2)}, u32[]{:S(2)}) collective-permute-start(bf16[512,256]{1,0:T(8,128)(2,1)S(1)} %add_convert_fusion.1.after_ref), channel_id=1, source_target_pairs={{0,4},{1,5},{2,6},{3,7},{4,0},{5,1},{6,2},{7,3},{8,12},{9,13},{10,... | collective-permute-start | bytes 786440 | tf_op jit(solution)/shard_map/reduce_cols/ppermute | solution.py:243
  66.7 6.3 %forward_part.7 = (bf16[512,256]{1,0:T(8,128)(2,1)}, bf16[512,256]{1,0:T(8,128)(2,1)}) custom-call(bf16[512,256]{1,0:T(8,128)(2,1)} %copy-done.15, bf16[4096,4096]{1,0:T(8,128)(2,1)} %build_dense.1.dense_ref, bf16[1024,256]{1,0:T(8,128)(2,1)} %copy-done.1, bf16[1024,256]{1,0:T(8,128)(2,1)} %copy-done.6, bf16[1024,256]{1,0:T(8,128)(2,1)} %copy-done.5, ...), custom_call_target="tpu_custom_call" | custom-call | flops 2147483648 | bytes 11534336 | tf_op jit(solution)/shard_map/forward/forward_part/pallas_call | solution.py:138
  74.1 6.3 %forward_part.5 = (bf16[512,256]{1,0:T(8,128)(2,1)}, bf16[512,256]{1,0:T(8,128)(2,1)}) custom-call(bf16[512,256]{1,0:T(8,128)(2,1)} %copy-done.16, bf16[4096,4096]{1,0:T(8,128)(2,1)} %build_dense.1.dense_ref, bf16[1024,256]{1,0:T(8,128)(2,1)} %copy-done.1, bf16[1024,256]{1,0:T(8,128)(2,1)} %copy-done.6, bf16[1024,256]{1,0:T(8,128)(2,1)} %copy-done.5, ...), custom_call_target="tpu_custom_call" | custom-call | flops 2147483648 | bytes 11534336 | tf_op jit(solution)/shard_map/forward/forward_part/pallas_call | solution.py:138
  80.7 2.6 %collective-permute-start.12 = (bf16[512,256]{1,0:T(8,128)(2,1)S(1)}, bf16[512,256]{1,0:T(8,128)(2,1)S(1)}, u32[]{:S(2)}, u32[]{:S(2)}) collective-permute-start(bf16[512,256]{1,0:T(8,128)(2,1)S(1)} %add_convert_fusion), channel_id=1, source_target_pairs={{0,6},{1,7},{2,0},{3,1},{4,2},{5,3},{6,4},{7,5},{8,14},{9,15},{10,... | collective-permute-start | bytes 786440 | tf_op jit(solution)/shard_map/reduce_cols/ppermute | solution.py:243
  83.3 6.0 %collective-permute-done.12 = bf16[512,256]{1,0:T(8,128)(2,1)S(1)} collective-permute-done((bf16[512,256]{1,0:T(8,128)(2,1)S(1)}, bf16[512,256]{1,0:T(8,128)(2,1)S(1)}, u32[]{:S(2)}, u32[]{:S(2)}) %collective-permute-start.12) | collective-permute-done | bytes 262176 | tf_op jit(solution)/shard_map/reduce_cols/ppermute | solution.py:243
  90.4 1.6 collective-permute-start.13
  92.0 3.4 %collective-permute-done.13 = bf16[256,256]{1,0:T(8,128)(2,1)S(1)} collective-permute-done((bf16[256,256]{1,0:T(8,128)(2,1)S(1)}, bf16[256,256]{1,0:T(8,128)(2,1)S(1)}, u32[]{:S(2)}, u32[]{:S(2)}) %collective-permute-start.13) | collective-permute-done | bytes 131104 | tf_op jit(solution)/shard_map/reduce_cols/ppermute | solution.py:247
  96.2 1.6 collective-permute-start.14
  98.0 3.2 %collective-permute-done.14 = bf16[256,256]{1,0:T(8,128)(2,1)S(1)} collective-permute-done((bf16[256,256]{1,0:T(8,128)(2,1)S(1)}, bf16[256,256]{1,0:T(8,128)(2,1)S(1)}, u32[]{:S(2)}, u32[]{:S(2)}) %collective-permute-start.14) | collective-permute-done | bytes 131104 | tf_op jit(solution)/shard_map/gather_slope/ppermute | solution.py:259
  101.3 1.4 collective-permute-start.20
  102.6 3.8 %collective-permute-start.18 = (bf16[512,256]{1,0:T(8,128)(2,1)S(1)}, bf16[512,256]{1,0:T(8,128)(2,1)S(1)}, u32[]{:S(2)}, u32[]{:S(2)}) collective-permute-start(bf16[512,256]{1,0:T(8,128)(2,1)S(1)} %pad_maximum_fusion.refs_0_), channel_id=1, source_target_pairs={{0,4},{1,5},{2,6},{3,7},{4,0},{5,1},{6,2},{7,3},{8,12},{9,13},{10,... | collective-permute-start | bytes 786440 | tf_op jit(solution)/shard_map/gather_slope/ppermute | solution.py:262
  107.4 7.4 %all-to-all-start = ((f32[16,16,256]{2,1,0:T(8,128)}), f32[16,16,256]{2,1,0:T(8,128)S(1)}, u32[]{:S(2)}, u32[]{:S(2)}) async-start(f32[16,16,256]{2,1,0:T(8,128)} %bitcast.2), calls=%async_computation | async-start | bytes 524288 | tf_op jit(solution)/shard_map/weight_grad/all_to_all | solution.py:266
  116.5 9.6 %all-to-all-done = f32[16,16,256]{2,1,0:T(8,128)S(1)} async-done(((f32[16,16,256]{2,1,0:T(8,128)}), f32[16,16,256]{2,1,0:T(8,128)S(1)}, u32[]{:S(2)}, u32[]{:S(2)}) %all-to-all-start) | async-done | bytes 262176 | tf_op jit(solution)/shard_map/weight_grad/all_to_all | solution.py:266
  127.0 6.2 %backward_part.5 = bf16[1024,256]{1,0:T(8,128)(2,1)} custom-call(f32[256,256]{1,0:T(8,128)} %bitcast.16, bf16[4096,4096]{1,0:T(8,128)(2,1)} %build_dense.1.dense_ref, bf16[512,256]{1,0:T(8,128)(2,1)} %copy-done.7, bf16[512,256]{1,0:T(8,128)(2,1)} %copy-done.11, bf16[512,256]{1,0:T(8,128)(2,1)} %copy-done.10, bf16[512,256]{1,0:T(8,128)(2,1)} %copy-done.14, ...), custom_call_target="tpu_custom_call" | custom-call | flops 2147483648 | bytes 11534336 | tf_op jit(solution)/shard_map/backward/backward_part/pallas_call | solution.py:170
  133.5 6.3 %backward_part.6 = bf16[1024,256]{1,0:T(8,128)(2,1)} custom-call(f32[256,256]{1,0:T(8,128)} %bitcast.17, bf16[4096,4096]{1,0:T(8,128)(2,1)} %build_dense.1.dense_ref, bf16[512,256]{1,0:T(8,128)(2,1)} %copy-done.7, bf16[512,256]{1,0:T(8,128)(2,1)} %copy-done.11, bf16[512,256]{1,0:T(8,128)(2,1)} %copy-done.10, bf16[512,256]{1,0:T(8,128)(2,1)} %copy-done.14, ...), custom_call_target="tpu_custom_call" | custom-call | flops 2147483648 | bytes 11534336 | tf_op jit(solution)/shard_map/backward/backward_part/pallas_call | solution.py:170
  139.8 2.3 %collective-permute-start.23 = (bf16[1024,256]{1,0:T(8,128)(2,1)}, bf16[1024,256]{1,0:T(8,128)(2,1)S(1)}, u32[]{:S(2)}, u32[]{:S(2)}) collective-permute-start(bf16[1024,256]{1,0:T(8,128)(2,1)} %backward_part.6), channel_id=1, source_target_pairs={{0,32},{16,48},{32,0},{48,16},{64,96},{80,112},{96,64},{112,80},{1... | collective-permute-start | bytes 1572872 | tf_op jit(solution)/shard_map/reduce_rows/ppermute | solution.py:272
  142.1 6.2 %backward_part.7 = bf16[1024,256]{1,0:T(8,128)(2,1)} custom-call(f32[256,256]{1,0:T(8,128)} %bitcast.18, bf16[4096,4096]{1,0:T(8,128)(2,1)} %build_dense.1.dense_ref, bf16[512,256]{1,0:T(8,128)(2,1)} %copy-done.7, bf16[512,256]{1,0:T(8,128)(2,1)} %copy-done.11, bf16[512,256]{1,0:T(8,128)(2,1)} %copy-done.10, bf16[512,256]{1,0:T(8,128)(2,1)} %copy-done.14, ...), custom_call_target="tpu_custom_call" | custom-call | flops 2147483648 | bytes 11534336 | tf_op jit(solution)/shard_map/backward/backward_part/pallas_call | solution.py:170
  148.4 1.8 collective-permute-start.24
  151.0 3.8 %all-to-all-start.1 = ((f32[16,1,256]{2,1,0:T(1,128)}), f32[16,1,256]{2,1,0:T(1,128)S(1)}, u32[]{:S(2)}, u32[]{:S(2)}) async-start(f32[16,1,256]{2,1,0:T(1,128)} %all_to_all.18), calls=%async_computation.1 | async-start | bytes 32768 | tf_op jit(solution)/shard_map/weight_grad/all_to_all | solution.py:283
  154.8 6.3 %backward_part.4 = bf16[1024,256]{1,0:T(8,128)(2,1)} custom-call(f32[256,256]{1,0:T(8,128)} %bitcast.19, bf16[4096,4096]{1,0:T(8,128)(2,1)} %build_dense.1.dense_ref, bf16[512,256]{1,0:T(8,128)(2,1)} %copy-done.7, bf16[512,256]{1,0:T(8,128)(2,1)} %copy-done.11, bf16[512,256]{1,0:T(8,128)(2,1)} %copy-done.10, bf16[512,256]{1,0:T(8,128)(2,1)} %copy-done.14, ...), custom_call_target="tpu_custom_call" | custom-call | flops 2147483648 | bytes 11534336 | tf_op jit(solution)/shard_map/backward/backward_part/pallas_call | solution.py:170
  164.6 3.0 %collective-permute-start.27 = (bf16[256,256]{1,0:T(8,128)(2,1)S(1)}, bf16[256,256]{1,0:T(8,128)(2,1)S(1)}, u32[]{:S(2)}, u32[]{:S(2)}) collective-permute-start(bf16[256,256]{1,0:T(8,128)(2,1)S(1)} %get-tuple-element.24), channel_id=1, source_target_pairs={{0,192},{16,208},{32,224},{48,240},{64,0},{80,16},{96,32},{112,48}... | collective-permute-start | bytes 393224 | tf_op jit(solution)/shard_map/reduce_rows/ppermute | solution.py:276
  167.7 1.6 collective-permute-start.26
  171.0 7.4 %collective-permute-done.25 = bf16[256,256]{1,0:T(8,128)(2,1)S(1)} collective-permute-done((bf16[256,256]{1,0:T(8,128)(2,1)S(1)}, bf16[256,256]{1,0:T(8,128)(2,1)S(1)}, u32[]{:S(2)}, u32[]{:S(2)}) %collective-permute-start.25) | collective-permute-done | bytes 131104 | tf_op jit(solution)/shard_map/reduce_rows/ppermute | solution.py:276
  (115 shorter events, 22.7 us)
Async XLA Ops:
  0.6 94.9 %copy-start = (bf16[256,256]{1,0:T(8,128)(2,1)S(1)}, bf16[256,256]{1,0:T(8,128)(2,1)}, u32[]{:S(2)}) copy-start(bf16[256,256]{1,0:T(8,128)(2,1)} %param.8) | copy-start | bytes 393220
  0.6 18.0 %collective-permute-start.1 = (bf16[256,256]{1,0:T(8,128)(2,1)}, bf16[256,256]{1,0:T(8,128)(2,1)S(1)}, u32[]{:S(2)}, u32[]{:S(2)}) collective-permute-start(bf16[256,256]{1,0:T(8,128)(2,1)} %param.7), channel_id=1, source_target_pairs={{0,128},{16,144},{32,160},{48,176},{64,192},{80,208},{96,224},{112... | collective-permute-start | bytes 393224 | tf_op jit(solution)/shard_map/gather_features/ppermute | solution.py:228
  7.0 11.6 %collective-permute-start = (bf16[256,256]{1,0:T(8,128)(2,1)}, bf16[256,256]{1,0:T(8,128)(2,1)S(1)}, u32[]{:S(2)}, u32[]{:S(2)}) collective-permute-start(bf16[256,256]{1,0:T(8,128)(2,1)} %param.7), channel_id=1, source_target_pairs={{0,192},{16,208},{32,224},{48,240},{64,0},{80,16},{96,32},{112,48}... | collective-permute-start | bytes 393224 | tf_op jit(solution)/shard_map/gather_features/ppermute | solution.py:228
  7.6 11.5 %collective-permute-start.2 = (bf16[256,256]{1,0:T(8,128)(2,1)}, bf16[256,256]{1,0:T(8,128)(2,1)S(1)}, u32[]{:S(2)}, u32[]{:S(2)}) collective-permute-start(bf16[256,256]{1,0:T(8,128)(2,1)} %param.7), channel_id=1, source_target_pairs={{0,64},{16,80},{32,96},{48,112},{64,128},{80,144},{96,160},{112,17... | collective-permute-start | bytes 393224 | tf_op jit(solution)/shard_map/gather_features/ppermute | solution.py:228
  19.1 29.7 %collective-permute-start.5 = (bf16[1024,256]{1,0:T(8,128)(2,1)S(1)}, bf16[1024,256]{1,0:T(8,128)(2,1)S(1)}, u32[]{:S(2)}, u32[]{:S(2)}) collective-permute-start(bf16[1024,256]{1,0:T(8,128)(2,1)S(1)} %constant_dynamic-update-slice_fusion.after_ref.refs_0_), channel_id=1, source_target_pairs={{0,16},{16,32},{32,48},{48,0},{64,80},{80,96},{96,112},{112,64},{1... | collective-permute-start | bytes 1572872 | tf_op jit(solution)/shard_map/gather_features/ppermute | solution.py:229
  20.7 28.0 %collective-permute-start.4 = (bf16[1024,256]{1,0:T(8,128)(2,1)S(1)}, bf16[1024,256]{1,0:T(8,128)(2,1)S(1)}, u32[]{:S(2)}, u32[]{:S(2)}) collective-permute-start(bf16[1024,256]{1,0:T(8,128)(2,1)S(1)} %constant_dynamic-update-slice_fusion.after_ref.refs_0_), channel_id=1, source_target_pairs={{0,32},{16,48},{32,0},{48,16},{64,96},{80,112},{96,64},{112,80},{1... | collective-permute-start | bytes 1572872 | tf_op jit(solution)/shard_map/gather_features/ppermute | solution.py:229
  23.6 25.1 %collective-permute-start.3 = (bf16[1024,256]{1,0:T(8,128)(2,1)S(1)}, bf16[1024,256]{1,0:T(8,128)(2,1)S(1)}, u32[]{:S(2)}, u32[]{:S(2)}) collective-permute-start(bf16[1024,256]{1,0:T(8,128)(2,1)S(1)} %constant_dynamic-update-slice_fusion.after_ref.refs_0_), channel_id=1, source_target_pairs={{0,48},{16,0},{32,16},{48,32},{64,112},{80,64},{96,80},{112,96},{1... | collective-permute-start | bytes 1572872 | tf_op jit(solution)/shard_map/gather_features/ppermute | solution.py:229
  56.8 6.8 %collective-permute-start.9 = (bf16[512,256]{1,0:T(8,128)(2,1)}, bf16[512,256]{1,0:T(8,128)(2,1)S(1)}, u32[]{:S(2)}, u32[]{:S(2)}) collective-permute-start(bf16[512,256]{1,0:T(8,128)(2,1)} %get-tuple-element.16), channel_id=1, source_target_pairs={{0,1},{1,0},{2,3},{3,2},{4,5},{5,4},{6,7},{7,6},{8,9},{9,8},{10,11... | collective-permute-start | bytes 786440 | tf_op jit(solution)/shard_map/reduce_cols/ppermute | solution.py:240
  63.2 9.8 %collective-permute-start.6 = (bf16[512,256]{1,0:T(8,128)(2,1)}, bf16[512,256]{1,0:T(8,128)(2,1)S(1)}, u32[]{:S(2)}, u32[]{:S(2)}) collective-permute-start(bf16[512,256]{1,0:T(8,128)(2,1)} %get-tuple-element.12), channel_id=1, source_target_pairs={{0,1},{1,0},{2,3},{3,2},{4,5},{5,4},{6,7},{7,6},{8,9},{9,8},{10,11... | collective-permute-start | bytes 786440 | tf_op jit(solution)/shard_map/reduce_cols/ppermute | solution.py:240
  63.7 19.5 %collective-permute-start.10 = (bf16[512,256]{1,0:T(8,128)(2,1)S(1)}, bf16[512,256]{1,0:T(8,128)(2,1)S(1)}, u32[]{:S(2)}, u32[]{:S(2)}) collective-permute-start(bf16[512,256]{1,0:T(8,128)(2,1)S(1)} %add_convert_fusion.1.after_ref), channel_id=1, source_target_pairs={{0,4},{1,5},{2,6},{3,7},{4,0},{5,1},{6,2},{7,3},{8,12},{9,13},{10,... | collective-permute-start | bytes 786440 | tf_op jit(solution)/shard_map/reduce_cols/ppermute | solution.py:243
  73.0 7.6 %collective-permute-start.11 = (bf16[512,256]{1,0:T(8,128)(2,1)}, bf16[512,256]{1,0:T(8,128)(2,1)S(1)}, u32[]{:S(2)}, u32[]{:S(2)}) collective-permute-start(bf16[512,256]{1,0:T(8,128)(2,1)} %get-tuple-element.18), channel_id=1, source_target_pairs={{0,1},{1,0},{2,3},{3,2},{4,5},{5,4},{6,7},{7,6},{8,9},{9,8},{10,11... | collective-permute-start | bytes 786440 | tf_op jit(solution)/shard_map/reduce_cols/ppermute | solution.py:240
  73.1 10.2 %collective-permute-start.8 = (bf16[512,256]{1,0:T(8,128)(2,1)S(1)}, bf16[512,256]{1,0:T(8,128)(2,1)S(1)}, u32[]{:S(2)}, u32[]{:S(2)}) collective-permute-start(bf16[512,256]{1,0:T(8,128)(2,1)S(1)} %add_convert_fusion.2.after_ref), channel_id=1, source_target_pairs={{0,2},{1,3},{2,4},{3,5},{4,6},{5,7},{6,0},{7,1},{8,10},{9,11},{10,... | collective-permute-start | bytes 786440 | tf_op jit(solution)/shard_map/reduce_cols/ppermute | solution.py:243
  80.4 2.9 %collective-permute-start.7 = (bf16[512,256]{1,0:T(8,128)(2,1)}, bf16[512,256]{1,0:T(8,128)(2,1)S(1)}, u32[]{:S(2)}, u32[]{:S(2)}) collective-permute-start(bf16[512,256]{1,0:T(8,128)(2,1)} %get-tuple-element.14), channel_id=1, source_target_pairs={{0,1},{1,0},{2,3},{3,2},{4,5},{5,4},{6,7},{7,6},{8,9},{9,8},{10,11... | collective-permute-start | bytes 786440 | tf_op jit(solution)/shard_map/reduce_cols/ppermute | solution.py:240
  80.7 8.6 %collective-permute-start.12 = (bf16[512,256]{1,0:T(8,128)(2,1)S(1)}, bf16[512,256]{1,0:T(8,128)(2,1)S(1)}, u32[]{:S(2)}, u32[]{:S(2)}) collective-permute-start(bf16[512,256]{1,0:T(8,128)(2,1)S(1)} %add_convert_fusion), channel_id=1, source_target_pairs={{0,6},{1,7},{2,0},{3,1},{4,2},{5,3},{6,4},{7,5},{8,14},{9,15},{10,... | collective-permute-start | bytes 786440 | tf_op jit(solution)/shard_map/reduce_cols/ppermute | solution.py:243
  90.4 5.1 %collective-permute-start.13 = (bf16[256,256]{1,0:T(8,128)(2,1)S(1)}, bf16[256,256]{1,0:T(8,128)(2,1)S(1)}, u32[]{:S(2)}, u32[]{:S(2)}) collective-permute-start(bf16[256,256]{1,0:T(8,128)(2,1)S(1)} %slice.50), channel_id=1, source_target_pairs={{0,8},{1,9},{2,10},{3,11},{4,12},{5,13},{6,14},{7,15},{8,0},{9,1},... | collective-permute-start | bytes 393224 | tf_op jit(solution)/shard_map/reduce_cols/ppermute | solution.py:247
  96.2 5.1 %collective-permute-start.14 = (bf16[256,256]{1,0:T(8,128)(2,1)S(1)}, bf16[256,256]{1,0:T(8,128)(2,1)S(1)}, u32[]{:S(2)}, u32[]{:S(2)}) collective-permute-start(bf16[256,256]{1,0:T(8,128)(2,1)S(1)} %fusion.1), channel_id=1, source_target_pairs={{0,8},{1,9},{2,10},{3,11},{4,12},{5,13},{6,14},{7,15},{8,0},{9,1},... | collective-permute-start | bytes 393224 | tf_op jit(solution)/shard_map/gather_slope/ppermute | solution.py:259
  101.2 24.8 %copy-start.7 = (bf16[512,256]{1,0:T(8,128)(2,1)}, bf16[512,256]{1,0:T(8,128)(2,1)S(1)}, u32[]{:S(2)}) copy-start(bf16[512,256]{1,0:T(8,128)(2,1)S(1)} %pad_maximum_fusion.refs_0_) | copy-start | bytes 786436
  101.3 13.7 %collective-permute-start.20 = (bf16[512,256]{1,0:T(8,128)(2,1)S(1)}, bf16[512,256]{1,0:T(8,128)(2,1)S(1)}, u32[]{:S(2)}, u32[]{:S(2)}) collective-permute-start(bf16[512,256]{1,0:T(8,128)(2,1)S(1)} %pad_maximum_fusion.refs_0_), channel_id=1, source_target_pairs={{0,2},{1,3},{2,4},{3,5},{4,6},{5,7},{6,0},{7,1},{8,10},{9,11},{10,... | collective-permute-start | bytes 786440 | tf_op jit(solution)/shard_map/gather_slope/ppermute | solution.py:262
  102.6 12.9 %collective-permute-start.18 = (bf16[512,256]{1,0:T(8,128)(2,1)S(1)}, bf16[512,256]{1,0:T(8,128)(2,1)S(1)}, u32[]{:S(2)}, u32[]{:S(2)}) collective-permute-start(bf16[512,256]{1,0:T(8,128)(2,1)S(1)} %pad_maximum_fusion.refs_0_), channel_id=1, source_target_pairs={{0,4},{1,5},{2,6},{3,7},{4,0},{5,1},{6,2},{7,3},{8,12},{9,13},{10,... | collective-permute-start | bytes 786440 | tf_op jit(solution)/shard_map/gather_slope/ppermute | solution.py:262
  106.5 9.1 %collective-permute-start.16 = (bf16[512,256]{1,0:T(8,128)(2,1)S(1)}, bf16[512,256]{1,0:T(8,128)(2,1)S(1)}, u32[]{:S(2)}, u32[]{:S(2)}) collective-permute-start(bf16[512,256]{1,0:T(8,128)(2,1)S(1)} %pad_maximum_fusion.refs_0_), channel_id=1, source_target_pairs={{0,6},{1,7},{2,0},{3,1},{4,2},{5,3},{6,4},{7,5},{8,14},{9,15},{10,... | collective-permute-start | bytes 786440 | tf_op jit(solution)/shard_map/gather_slope/ppermute | solution.py:262
  107.4 18.6 %all-to-all-start = ((f32[16,16,256]{2,1,0:T(8,128)}), f32[16,16,256]{2,1,0:T(8,128)S(1)}, u32[]{:S(2)}, u32[]{:S(2)}) async-start(f32[16,16,256]{2,1,0:T(8,128)} %bitcast.2), calls=%async_computation | async-start | bytes 524288 | tf_op jit(solution)/shard_map/weight_grad/all_to_all | solution.py:266
  114.9 1.6 collective-permute-start.15
  115.0 11.1 %collective-permute-start.21 = (bf16[512,256]{1,0:T(8,128)(2,1)S(1)}, bf16[512,256]{1,0:T(8,128)(2,1)S(1)}, u32[]{:S(2)}, u32[]{:S(2)}) collective-permute-start(bf16[512,256]{1,0:T(8,128)(2,1)S(1)} %collective-permute-done.20.refs_6_), channel_id=1, source_target_pairs={{0,1},{1,0},{2,3},{3,2},{4,5},{5,4},{6,7},{7,6},{8,9},{9,8},{10,11... | collective-permute-start | bytes 786440 | tf_op jit(solution)/shard_map/gather_slope/ppermute | solution.py:263
  115.5 10.5 %collective-permute-start.19 = (bf16[512,256]{1,0:T(8,128)(2,1)S(1)}, bf16[512,256]{1,0:T(8,128)(2,1)S(1)}, u32[]{:S(2)}, u32[]{:S(2)}) collective-permute-start(bf16[512,256]{1,0:T(8,128)(2,1)S(1)} %collective-permute-done.18.refs_4_), channel_id=1, source_target_pairs={{0,1},{1,0},{2,3},{3,2},{4,5},{5,4},{6,7},{7,6},{8,9},{9,8},{10,11... | collective-permute-start | bytes 786440 | tf_op jit(solution)/shard_map/gather_slope/ppermute | solution.py:263
  115.6 10.5 %collective-permute-start.17 = (bf16[512,256]{1,0:T(8,128)(2,1)S(1)}, bf16[512,256]{1,0:T(8,128)(2,1)S(1)}, u32[]{:S(2)}, u32[]{:S(2)}) collective-permute-start(bf16[512,256]{1,0:T(8,128)(2,1)S(1)} %collective-permute-done.16.refs_2_), channel_id=1, source_target_pairs={{0,1},{1,0},{2,3},{3,2},{4,5},{5,4},{6,7},{7,6},{8,9},{9,8},{10,11... | collective-permute-start | bytes 786440 | tf_op jit(solution)/shard_map/gather_slope/ppermute | solution.py:263
  133.3 27.8 %collective-permute-start.22 = (bf16[1024,256]{1,0:T(8,128)(2,1)}, bf16[1024,256]{1,0:T(8,128)(2,1)S(1)}, u32[]{:S(2)}, u32[]{:S(2)}) collective-permute-start(bf16[1024,256]{1,0:T(8,128)(2,1)} %backward_part.5), channel_id=1, source_target_pairs={{0,16},{16,32},{32,48},{48,0},{64,80},{80,96},{96,112},{112,64},{1... | collective-permute-start | bytes 1572872 | tf_op jit(solution)/shard_map/reduce_rows/ppermute | solution.py:272
  139.8 21.3 %collective-permute-start.23 = (bf16[1024,256]{1,0:T(8,128)(2,1)}, bf16[1024,256]{1,0:T(8,128)(2,1)S(1)}, u32[]{:S(2)}, u32[]{:S(2)}) collective-permute-start(bf16[1024,256]{1,0:T(8,128)(2,1)} %backward_part.6), channel_id=1, source_target_pairs={{0,32},{16,48},{32,0},{48,16},{64,96},{80,112},{96,64},{112,80},{1... | collective-permute-start | bytes 1572872 | tf_op jit(solution)/shard_map/reduce_rows/ppermute | solution.py:272
  148.4 13.8 %collective-permute-start.24 = (bf16[1024,256]{1,0:T(8,128)(2,1)}, bf16[1024,256]{1,0:T(8,128)(2,1)S(1)}, u32[]{:S(2)}, u32[]{:S(2)}) collective-permute-start(bf16[1024,256]{1,0:T(8,128)(2,1)} %backward_part.7), channel_id=1, source_target_pairs={{0,48},{16,0},{32,16},{48,32},{64,112},{80,64},{96,80},{112,96},{1... | collective-permute-start | bytes 1572872 | tf_op jit(solution)/shard_map/reduce_rows/ppermute | solution.py:272
  151.0 19.3 %all-to-all-start.1 = ((f32[16,1,256]{2,1,0:T(1,128)}), f32[16,1,256]{2,1,0:T(1,128)S(1)}, u32[]{:S(2)}, u32[]{:S(2)}) async-start(f32[16,1,256]{2,1,0:T(1,128)} %all_to_all.18), calls=%async_computation.1 | async-start | bytes 32768 | tf_op jit(solution)/shard_map/weight_grad/all_to_all | solution.py:283
  163.5 15.0 %collective-permute-start.25 = (bf16[256,256]{1,0:T(8,128)(2,1)S(1)}, bf16[256,256]{1,0:T(8,128)(2,1)S(1)}, u32[]{:S(2)}, u32[]{:S(2)}) collective-permute-start(bf16[256,256]{1,0:T(8,128)(2,1)S(1)} %get-tuple-element.23), channel_id=1, source_target_pairs={{0,64},{16,80},{32,96},{48,112},{64,128},{80,144},{96,160},{112,17... | collective-permute-start | bytes 393224 | tf_op jit(solution)/shard_map/reduce_rows/ppermute | solution.py:276
  164.6 13.8 %collective-permute-start.27 = (bf16[256,256]{1,0:T(8,128)(2,1)S(1)}, bf16[256,256]{1,0:T(8,128)(2,1)S(1)}, u32[]{:S(2)}, u32[]{:S(2)}) collective-permute-start(bf16[256,256]{1,0:T(8,128)(2,1)S(1)} %get-tuple-element.24), channel_id=1, source_target_pairs={{0,192},{16,208},{32,224},{48,240},{64,0},{80,16},{96,32},{112,48}... | collective-permute-start | bytes 393224 | tf_op jit(solution)/shard_map/reduce_rows/ppermute | solution.py:276
  167.7 11.7 %collective-permute-start.26 = (bf16[256,256]{1,0:T(8,128)(2,1)S(1)}, bf16[256,256]{1,0:T(8,128)(2,1)S(1)}, u32[]{:S(2)}, u32[]{:S(2)}) collective-permute-start(bf16[256,256]{1,0:T(8,128)(2,1)S(1)} %get-tuple-element.25), channel_id=1, source_target_pairs={{0,128},{16,144},{32,160},{48,176},{64,192},{80,208},{96,224},{112... | collective-permute-start | bytes 393224 | tf_op jit(solution)/shard_map/reduce_rows/ppermute | solution.py:276
  (20 other events, 124.8 us)
